TPU v7x, 512 devices: a whole 4x4x16 slice. The times are simulated.
512 devices in a mesh: seq: 128 (over y, x_hi, z), chan: 4 (over x_lo, core).
Axes of the slice: x: 4 (x_hi: 2, x_lo: 2; x = x_hi * 2 + x_lo), y: 4, z: 16, core: 2. Of those that a mesh axis runs over, the one named last changes fastest.
Arguments:
- inputs: bfloat16 [128, 32768], P('chan', 'seq'), may hold values from -6 to 6
- gate_values: bfloat16 [128, 32768], P('chan', 'seq'), may hold values from -6 to 6
- filters: float32 [8, 32768], P('chan', 'seq'), may hold values from -5 to 5
- skip_weight: float32 [128], P('chan'), may hold values from -4 to 4
- grad_out: bfloat16 [128, 32768], P('chan', 'seq'), may hold values from -6 to 6
Outputs:
- grad_input: bfloat16 [128, 32768], P('chan', 'seq')
- grad_gate: bfloat16 [128, 32768], P('chan', 'seq')
- grad_filter: float32 [8, 32768], P('chan', 'seq')
All inputs are finite; a program needn't handle non-finite values.
Results may differ from a plain program's by a relative error of at most 0.0014.
Values sent between devices are 32-bit elements; how exact they have to be, the bound alone decides.
No kernel may reach another device: no remote copies, remote signals or barrier semaphores. Data moves between devices by JAX's collectives and lax.ppermute only.
A program may use at most 64 MiB of HBM per device.

v0:
```python
import math

import jax
import jax.numpy as jnp
from jax import lax
from jax.experimental import pallas as pl
from jax.experimental.pallas import tpu as pltpu
from jax.sharding import PartitionSpec as P

BLOCK = 256
BLOCKS = 128
QUARTERS = 4
FINE = 16
PARTS = BLOCK // (QUARTERS * FINE)
STEPS = BLOCKS // FINE
F32 = jnp.float32
BF16 = jnp.bfloat16


def split(value):
    high = value.astype(BF16)
    return high, (value - high.astype(F32)).astype(BF16)


def rows_down(value):
    row = lax.broadcasted_iota(jnp.int32, value.shape, 0)
    return jnp.where(row == 0, 0.0, pltpu.roll(value, 1, 0))


def rows_up(value):
    row = lax.broadcasted_iota(jnp.int32, value.shape, 0)
    return jnp.where(row == BLOCKS - 1, 0.0, pltpu.roll(value, BLOCKS - 1, 0))


def nt_dot(left, right):
    return lax.dot_general(
        left, right, (((1,), (1,)), ((), ())), preferred_element_type=F32
    )


def window_rows(wide, start, store):
    turned = pltpu.roll(wide, (2 * BLOCK - start) % (2 * BLOCK), 1)
    half = pltpu.roll(turned, 2 * BLOCK - BLOCK // PARTS, 1)
    store(0, turned[:, :BLOCK])
    store(1, half[:, :BLOCK])
    store(2, turned[:, 128 : 128 + BLOCK])
    store(3, half[:, 128 : 128 + BLOCK])


def middle_kernel(r_ref, a_ref, out_ref, taps, windows, acc):
    r = r_ref[0]
    x = jnp.concatenate([a_ref[0], a_ref[1]], axis=1)
    g = jnp.concatenate([a_ref[2], a_ref[3]], axis=1)
    h = jnp.concatenate([a_ref[4], a_ref[5]], axis=1)
    h_down = rows_down(h)

    def keep(slot):
        def store(i, rows):
            high, low = split(rows)
            windows[slot, i] = high
            windows[slot + 1, i] = low

        return store

    window_rows(jnp.concatenate([g, rows_up(g)], axis=1), FINE * r, keep(0))
    window_rows(jnp.concatenate([h_down, h], axis=1), FINE * r + FINE, keep(2))

    def taps_of(slot, wide, shift_of, low_slot=None):
        for n in range(FINE):
            turned = pltpu.roll(wide, shift_of(n) % 384, 1) if shift_of(n) % 384 else wide
            value = turned[:, 128:]
            high, low = split(value)
            taps[slot, :, n] = high.reshape(STEPS, FINE, BLOCK)
            if low_slot is not None:
                taps[low_slot, :, n] = low.reshape(STEPS, FINE, BLOCK)

    x_down = rows_down(x)
    taps_of(0, jnp.concatenate([h_down[:, 128:], h], axis=1), lambda n: n, 1)
    taps_of(2, jnp.concatenate([x_down[:, 128:], x], axis=1), lambda n: n)
    lane = lax.broadcasted_iota(jnp.int32, (BLOCK, BLOCK), 1)
    row = lax.broadcasted_iota(jnp.int32, (BLOCK, BLOCK), 0)
    mirror = (lane + row == BLOCK - 1).astype(BF16)
    flipped = jnp.dot(x.astype(BF16), mirror, preferred_element_type=F32)
    flipped_down = rows_down(flipped)
    wide = jnp.concatenate([flipped, flipped_down[:, :128]], axis=1)
    taps_of(3, pltpu.roll(wide, 128, 1), lambda n: n - (FINE - 1))

    for step in range(STEPS):
        shift = FINE * step
        size = BLOCKS - shift

        def rhs(slot):
            return taps[slot, step].reshape(BLOCK, BLOCK)

        def lhs(slot, start):
            return windows[slot, :, start : start + size].reshape(PARTS * size, BLOCK)

        g_high, g_low = lhs(0, shift), lhs(1, shift)
        h_high, h_low = lhs(2, 0), lhs(3, 0)
        cross = nt_dot(g_high, rhs(2)) + nt_dot(g_low, rhs(2))
        pulled = nt_dot(g_high, rhs(0)) + nt_dot(g_low, rhs(0)) + nt_dot(g_high, rhs(1))
        conv = nt_dot(h_high, rhs(3)) + nt_dot(h_low, rhs(3))
        for slot, start, value in ((0, shift, conv), (1, 0, pulled), (2, 0, cross)):
            value = value.reshape(PARTS, size, BLOCK)
            if step == 0:
                acc[slot] = value
            else:
                acc[slot, :, start : start + size] = acc[slot, :, start : start + size] + value

    column = lax.broadcasted_iota(jnp.int32, (BLOCKS, BLOCK), 1) % FINE
    line = lax.broadcasted_iota(jnp.int32, (BLOCKS, BLOCK), 0)
    source = lax.broadcasted_iota(jnp.int32, (BLOCK, 128), 0)
    target = lax.broadcasted_iota(jnp.int32, (BLOCK, 128), 1)
    totals = [jnp.zeros((BLOCKS, 128), F32), jnp.zeros((BLOCKS, 128), F32)]
    for slot, page, offset in ((0, 0, 0), (1, 0, 64), (2, 1, 0)):
        total = totals[page]
        for i in range(PARTS):
            value = acc[slot, i]
            for bit in (1, 2, 4, 8):
                if slot == 0:
                    moved = jnp.where(line < bit, 0.0, pltpu.roll(value, bit, 0))
                else:
                    moved = jnp.where(line >= BLOCKS - bit, 0.0, pltpu.roll(value, BLOCKS - bit, 0))
                value = jnp.where((column & bit) != 0, moved, value)
            pick = (source // FINE + FINE * i + offset == target).astype(BF16)
            high, low = split(value)
            total = total + jnp.dot(high, pick, preferred_element_type=F32)
            total = total + jnp.dot(low, pick, preferred_element_type=F32)
        totals[page] = total
    out_ref[0] = totals[0]
    out_ref[1] = totals[1]


def middle(arrived, r):
    return pl.pallas_call(
        middle_kernel,
        out_shape=jax.ShapeDtypeStruct((2, BLOCKS, 128), F32),
        in_specs=[
            pl.BlockSpec(memory_space=pltpu.SMEM),
            pl.BlockSpec(memory_space=pltpu.VMEM),
        ],
        out_specs=pl.BlockSpec(memory_space=pltpu.VMEM),
        scratch_shapes=[
            pltpu.VMEM((4, STEPS, FINE, FINE, BLOCK), BF16),
            pltpu.VMEM((4, PARTS, BLOCKS, BLOCK), BF16),
            pltpu.VMEM((3, PARTS, BLOCKS, BLOCK), F32),
        ],
        compiler_params=pltpu.CompilerParams(vmem_limit_bytes=48 * 1024 * 1024),
    )(r, arrived)


def source_kernel(x_ref, gate_ref, up_ref, filter_ref, out_ref):
    x = x_ref[...].astype(F32)
    mixed = up_ref[...].astype(F32) * gate_ref[...].astype(F32)
    filters = jnp.concatenate([filter_ref[...]] * 4, axis=0)
    for page, value in ((0, x), (2, mixed), (4, filters)):
        for half in range(2):
            part = value[:, 128 * half : 128 * half + 128]
            for quarter in range(QUARTERS):
                out_ref[page + half, 32 * quarter : 32 * quarter + 32] = part


def source(x, gate, up, filters):
    return pl.pallas_call(
        source_kernel,
        out_shape=jax.ShapeDtypeStruct((6, BLOCKS, 128), F32),
    )(x, gate, up, filters)


def exact_dot(value, pick):
    high = value.astype(BF16)
    rest = value - high.astype(F32)
    mid = rest.astype(BF16)
    low = (rest - mid.astype(F32)).astype(BF16)
    total = jnp.dot(high, pick, preferred_element_type=F32)
    total = total + jnp.dot(mid, pick, preferred_element_type=F32)
    return total + jnp.dot(low, pick, preferred_element_type=F32)


def final_kernel(b_ref, x_ref, gate_ref, up_ref, skip_ref, gi_ref, gg_ref, gf_ref):
    source = lax.broadcasted_iota(jnp.int32, (128, 2 * BLOCK), 0)
    target = lax.broadcasted_iota(jnp.int32, (128, 2 * BLOCK), 1)
    both = jnp.zeros((32, 2 * BLOCK), F32)
    taps = jnp.zeros((8, BLOCK), F32)
    for quarter in range(QUARTERS):
        place = (source // FINE) * (BLOCK // PARTS) + FINE * quarter + source % FINE
        pick = (place == target).astype(BF16)
        both = both + exact_dot(b_ref[0, 32 * quarter : 32 * quarter + 32], pick)
        cross = b_ref[1, 32 * quarter : 32 * quarter + 32].reshape(4, 8, 128).sum(axis=0)
        taps = taps + exact_dot(cross, pick[:, :BLOCK])
    x = x_ref[...].astype(F32)
    up = up_ref[...].astype(F32)
    mixed = up * gate_ref[...].astype(F32)
    skip = skip_ref[...]
    gg_ref[...] = (up * (both[:, :BLOCK] + skip * x)).astype(BF16)
    gi_ref[...] = (both[:, BLOCK:] + skip * mixed).astype(BF16)
    gf_ref[...] = taps * (1.0 / math.sqrt(BLOCKS * BLOCK))


def final(returned, x, gate, up, skip):
    piece = jax.ShapeDtypeStruct((32, BLOCK), BF16)
    return pl.pallas_call(
        final_kernel,
        out_shape=(piece, piece, jax.ShapeDtypeStruct((8, BLOCK), F32)),
    )(returned, x, gate, up, skip)


def body(inputs, gate_values, filters, skip_weight, grad_out):
    quarter = (lax.axis_index("seq") // 32).astype(jnp.int32).reshape(1)
    every_filter = lax.all_gather(filters, "chan", axis=0, tiled=True)
    leaving = source(inputs, gate_values, grad_out, every_filter)
    arrived = lax.all_to_all(leaving, "seq", split_axis=1, concat_axis=1, tiled=True)
    results = middle(arrived, quarter)
    returned = lax.all_to_all(results, "seq", split_axis=1, concat_axis=1, tiled=True)
    grad_input, grad_gate, taps = final(
        returned, inputs, gate_values, grad_out, skip_weight[:, None]
    )
    grad_filter = lax.psum_scatter(taps, "chan", scatter_dimension=0, tiled=True)
    return (grad_input, grad_gate, grad_filter)


def solution(mesh):
    placed = (P("chan", "seq"), P("chan", "seq"), P("chan", "seq"), P("chan"), P("chan", "seq"))
    return jax.shard_map(
        body,
        mesh=mesh,
        in_specs=placed,
        out_specs=(P("chan", "seq"), P("chan", "seq"), P("chan", "seq")),
        check_vma=False,
    )
```

profile of v0, /device:TPU:1, one launch (start us, length us, event | category | flops | bytes accessed | tf_op | source)
XLA Modules:
  0.0 108.9 jit_solution(14868708618897219402)
XLA Ops:
  0.6 12.0 %all-gather = f32[4,2,256]{2,1,0:T(2,128)S(1)} all-gather(f32[1,2,256]{2,1,0:T(2,128)} %bitcast.4), channel_id=1, replica_groups=mesh['seq'=128,'chan'=4] {'chan'}, dimensions={0}, use_global_device_ids=true | all-gather | bytes 10240 | tf_op jit(solution)/shard_map/all_gather | solution.py:210
  12.6 0.6 reshape.11.filter_ref
  13.2 1.5 %shard_map.76 = f32[6,128,128]{2,1,0:T(8,128)} custom-call(bf16[32,256]{1,0:T(8,128)(2,1)} %x_ref.3, bf16[32,256]{1,0:T(8,128)(2,1)} %gate_ref.3, bf16[32,256]{1,0:T(8,128)(2,1)} %up_ref.3, f32[8,256]{1,0:T(8,128)} %reshape.11.filter_ref), custom_call_target="tpu_custom_call" | custom-call | tf_op jit(solution)/shard_map/pallas_call | solution.py:164
  14.7 2.0 %copy.9 = f32[6,128,128]{2,0,1:T(8,128)} copy(f32[6,128,128]{2,1,0:T(8,128)} %shard_map.76) | data formatting | bytes 786432 | tf_op jit(solution)/shard_map/pallas_call | solution.py:164
  16.8 16.8 %all-to-all-start = ((f32[6,128,128]{2,0,1:T(8,128)}), f32[6,128,128]{2,0,1:T(8,128)S(1)}, u32[]{:S(2)}, u32[]{:S(2)}) async-start(f32[6,128,128]{2,0,1:T(8,128)} %copy.9), calls=%async_computation | async-start | bytes 1048576 | tf_op jit(solution)/shard_map/all_to_all | solution.py:212
  33.5 32.2 %all-to-all-done = f32[6,128,128]{2,0,1:T(8,128)S(1)} async-done(((f32[6,128,128]{2,0,1:T(8,128)}), f32[6,128,128]{2,0,1:T(8,128)S(1)}, u32[]{:S(2)}, u32[]{:S(2)}) %all-to-all-start) | async-done | bytes 393248 | tf_op jit(solution)/shard_map/all_to_all | solution.py:212
  65.8 0.1 copy.10.a_ref
  65.9 4.2 %shard_map.77 = f32[2,128,128]{2,1,0:T(8,128)S(1)} custom-call(s32[1]{0:T(128)} %bitcast.r_ref, f32[6,128,128]{2,1,0:T(8,128)S(1)} %copy.10.a_ref), custom_call_target="tpu_custom_call" | custom-call | tf_op jit(solution)/shard_map/pallas_call | solution.py:135
  70.1 0.7 copy.11
  70.8 9.1 %all-to-all-start.1 = ((f32[2,128,128]{2,0,1:T(2,128)}), f32[2,128,128]{2,0,1:T(2,128)S(1)}, u32[]{:S(2)}, u32[]{:S(2)}) async-start(f32[2,128,128]{2,0,1:T(2,128)} %copy.11), calls=%async_computation.1 | async-start | bytes 262144 | tf_op jit(solution)/shard_map/all_to_all | solution.py:214
  80.0 0.0 copy-start
  80.0 0.6 copy-done
  80.6 0.7 copy.13.skip_ref
  81.3 1.3 %dynamic-slice = u32[1]{0:T(128)} dynamic-slice(u32[512]{0:T(512)} %constant.25, u32[]{:T(128)S(6)} %add.4), dynamic_slice_sizes={1} | dynamic-slice | bytes 12
  83.2 13.8 %all-to-all-done.1 = f32[2,128,128]{2,0,1:T(2,128)S(1)} async-done(((f32[2,128,128]{2,0,1:T(2,128)}), f32[2,128,128]{2,0,1:T(2,128)S(1)}, u32[]{:S(2)}, u32[]{:S(2)}) %all-to-all-start.1) | async-done | bytes 131104 | tf_op jit(solution)/shard_map/all_to_all | solution.py:214
  97.0 0.7 copy.12.b_ref
  97.7 2.0 %shard_map.78 = (bf16[32,256]{1,0:T(8,128)(2,1)}, bf16[32,256]{1,0:T(8,128)(2,1)}, f32[8,256]{1,0:T(8,128)}) custom-call(f32[2,128,128]{2,1,0:T(8,128)} %copy.12.b_ref, bf16[32,256]{1,0:T(8,128)(2,1)} %x_ref.3, bf16[32,256]{1,0:T(8,128)(2,1)} %gate_ref.3, bf16[32,256]{1,0:T(8,128)(2,1)} %up_ref.3, f32[32,1]{1,0:T(8,128)} %copy.13.skip_ref), custom_call_target="tpu_custom_call" | custom-call | tf_op jit(solution)/shard_map/pallas_call | solution.py:202
  99.7 8.6 %all-reduce = f32[8,256]{1,0:T(8,128)S(1)} all-reduce(f32[8,256]{1,0:T(8,128)} %get-tuple-element.8), channel_id=2, replica_groups=mesh['seq'=128,'chan'=4] {'chan'}, use_global_device_ids=true, to_apply=%region_0.1.clone | all-reduce | flops 2048 | bytes 16384
  108.3 0.6 constant_dynamic-slice_fusion
Async XLA Ops:
  16.8 49.0 %all-to-all-start = ((f32[6,128,128]{2,0,1:T(8,128)}), f32[6,128,128]{2,0,1:T(8,128)S(1)}, u32[]{:S(2)}, u32[]{:S(2)}) async-start(f32[6,128,128]{2,0,1:T(8,128)} %copy.9), calls=%async_computation | async-start | bytes 1048576 | tf_op jit(solution)/shard_map/all_to_all | solution.py:212
  70.8 26.2 %all-to-all-start.1 = ((f32[2,128,128]{2,0,1:T(2,128)}), f32[2,128,128]{2,0,1:T(2,128)S(1)}, u32[]{:S(2)}, u32[]{:S(2)}) async-start(f32[2,128,128]{2,0,1:T(2,128)} %copy.11), calls=%async_computation.1 | async-start | bytes 262144 | tf_op jit(solution)/shard_map/all_to_all | solution.py:214
  80.0 0.7 copy-start
where the time goes:
time: 109 us
  waiting for transfers between devices  46 us (42%)
  starting transfers between devices  25.9 us (24%)
  blocking collectives  20.6 us (19%)
  Pallas kernels  7.7 us (7%)
  local copies, waits for them, and re-layouts  7.29 us (7%)
  between operations  1.35 us (1%)
    all_to_all x1, waiting for transfers between devices, body(): lax.all_to_all(leaving, 'seq', split_axis=1, concat_axis=1, tiled=True)  32.2 us
    all_to_all x1, starting transfers between devices, body(): lax.all_to_all(leaving, 'seq', split_axis=1, concat_axis=1, tiled=True)  16.8 us
    all_to_all x1, waiting for transfers between devices, body(): lax.all_to_all(results, 'seq', split_axis=1, concat_axis=1, tiled=True)  13.8 us
    all_gather x1, blocking collectives, body(): every_filter = lax.all_gather(filters, 'chan', axis=0, tiled=True)  12 us
    all_to_all x1, starting transfers between devices, body(): lax.all_to_all(results, 'seq', split_axis=1, concat_axis=1, tiled=True)  9.14 us
    unnamed x1, blocking collectives  8.65 us
    pallas_call x1, Pallas kernels, middle(): pl.pallas_call(middle_kernel, out_shape=jax.ShapeDtypeStruct((2, BLOCKS,...  4.19 us
    unnamed x5, local copies, waits for them, and re-layouts  3.11 us
  transfers between devices with their start and end apart: 2, of which 2 were waited for; matrix products, arithmetic and copies ran while one was open for 2% of the time, Pallas kernels for 0%

commit v1 on v0

--- a/solution.py
+++ b/solution.py
@@ -49,9 +49,12 @@
 
 def middle_kernel(r_ref, a_ref, out_ref, taps, windows, acc):
     r = r_ref[0]
-    x = jnp.concatenate([a_ref[0], a_ref[1]], axis=1)
-    g = jnp.concatenate([a_ref[2], a_ref[3]], axis=1)
-    h = jnp.concatenate([a_ref[4], a_ref[5]], axis=1)
+
+    def signal(first):
+        halves = [a_ref[:, first + half].reshape(BLOCKS, 128) for half in range(2)]
+        return jnp.concatenate(halves, axis=1)
+
+    x, g, h = signal(0), signal(2), signal(4)
     h_down = rows_down(h)
 
     def keep(slot):
@@ -127,14 +130,14 @@
             total = total + jnp.dot(high, pick, preferred_element_type=F32)
             total = total + jnp.dot(low, pick, preferred_element_type=F32)
         totals[page] = total
-    out_ref[0] = totals[0]
-    out_ref[1] = totals[1]
+    out_ref[:, 0] = totals[0]
+    out_ref[:, 1] = totals[1]
 
 
 def middle(arrived, r):
     return pl.pallas_call(
         middle_kernel,
-        out_shape=jax.ShapeDtypeStruct((2, BLOCKS, 128), F32),
+        out_shape=jax.ShapeDtypeStruct((BLOCKS, 2, 128), F32),
         in_specs=[
             pl.BlockSpec(memory_space=pltpu.SMEM),
             pl.BlockSpec(memory_space=pltpu.VMEM),
@@ -149,22 +152,43 @@
     )(r, arrived)
 
 
+RING = 16
+PLANES = 8
+
+
 def source_kernel(x_ref, gate_ref, up_ref, filter_ref, out_ref):
     x = x_ref[...].astype(F32)
     mixed = up_ref[...].astype(F32) * gate_ref[...].astype(F32)
-    filters = jnp.concatenate([filter_ref[...]] * 4, axis=0)
-    for page, value in ((0, x), (2, mixed), (4, filters)):
+    filters = jnp.concatenate([filter_ref[i] for i in range(4)] * 2, axis=0)
+    line = 0
+    for value in (x[:RING], x[RING:], mixed[:RING], mixed[RING:], filters):
         for half in range(2):
-            part = value[:, 128 * half : 128 * half + 128]
-            for quarter in range(QUARTERS):
-                out_ref[page + half, 32 * quarter : 32 * quarter + 32] = part
+            out_ref[:, line] = value[:, 128 * half : 128 * half + 128]
+            line += 1
+    out_ref[:, line:] = jnp.zeros((RING, 16 - line, 128), F32)
 
 
 def source(x, gate, up, filters):
     return pl.pallas_call(
         source_kernel,
-        out_shape=jax.ShapeDtypeStruct((6, BLOCKS, 128), F32),
+        out_shape=jax.ShapeDtypeStruct((RING, 16, 128), F32),
     )(x, gate, up, filters)
+
+
+def spread_kernel(in_ref, out_ref):
+    lines = [in_ref[:, line] for line in range(10)]
+    for plane in range(PLANES):
+        member = plane % 2
+        chosen = (2 * member, 2 * member + 1, 4 + 2 * member, 5 + 2 * member, 8, 9)
+        for place, line in enumerate(chosen):
+            out_ref[plane, place] = lines[line]
+
+
+def spread(ring):
+    return pl.pallas_call(
+        spread_kernel,
+        out_shape=jax.ShapeDtypeStruct((PLANES, 6, RING, 128), F32),
+    )(ring)
 
 
 def exact_dot(value, pick):
@@ -177,45 +201,64 @@
     return total + jnp.dot(low, pick, preferred_element_type=F32)
 
 
-def final_kernel(b_ref, x_ref, gate_ref, up_ref, skip_ref, gi_ref, gg_ref, gf_ref):
-    source = lax.broadcasted_iota(jnp.int32, (128, 2 * BLOCK), 0)
-    target = lax.broadcasted_iota(jnp.int32, (128, 2 * BLOCK), 1)
-    both = jnp.zeros((32, 2 * BLOCK), F32)
+def quarter_pick(quarter, width):
+    source = lax.broadcasted_iota(jnp.int32, (128, width), 0)
+    target = lax.broadcasted_iota(jnp.int32, (128, width), 1)
+    place = (source // FINE) * (BLOCK // PARTS) + FINE * quarter + source % FINE
+    return (place == target).astype(BF16)
+
+
+def taps_kernel(b_ref, gf_ref):
     taps = jnp.zeros((8, BLOCK), F32)
     for quarter in range(QUARTERS):
-        place = (source // FINE) * (BLOCK // PARTS) + FINE * quarter + source % FINE
-        pick = (place == target).astype(BF16)
-        both = both + exact_dot(b_ref[0, 32 * quarter : 32 * quarter + 32], pick)
-        cross = b_ref[1, 32 * quarter : 32 * quarter + 32].reshape(4, 8, 128).sum(axis=0)
-        taps = taps + exact_dot(cross, pick[:, :BLOCK])
+        cross = b_ref[32 * quarter : 32 * quarter + 32, 1].reshape(4, 8, 128).sum(axis=0)
+        taps = taps + exact_dot(cross, quarter_pick(quarter, BLOCK))
+    gf_ref[...] = taps * (1.0 / math.sqrt(BLOCKS * BLOCK))
+
+
+def final_taps(returned):
+    return pl.pallas_call(
+        taps_kernel, out_shape=jax.ShapeDtypeStruct((8, BLOCK), F32)
+    )(returned)
+
+
+def final_kernel(b_ref, x_ref, gate_ref, up_ref, skip_ref, gi_ref, gg_ref):
+    both = jnp.zeros((32, 2 * BLOCK), F32)
+    for quarter in range(QUARTERS):
+        rows = b_ref[32 * quarter : 32 * quarter + 32, 0]
+        both = both + exact_dot(rows, quarter_pick(quarter, 2 * BLOCK))
     x = x_ref[...].astype(F32)
     up = up_ref[...].astype(F32)
     mixed = up * gate_ref[...].astype(F32)
     skip = skip_ref[...]
     gg_ref[...] = (up * (both[:, :BLOCK] + skip * x)).astype(BF16)
     gi_ref[...] = (both[:, BLOCK:] + skip * mixed).astype(BF16)
-    gf_ref[...] = taps * (1.0 / math.sqrt(BLOCKS * BLOCK))
 
 
 def final(returned, x, gate, up, skip):
     piece = jax.ShapeDtypeStruct((32, BLOCK), BF16)
-    return pl.pallas_call(
-        final_kernel,
-        out_shape=(piece, piece, jax.ShapeDtypeStruct((8, BLOCK), F32)),
-    )(returned, x, gate, up, skip)
+    return pl.pallas_call(final_kernel, out_shape=(piece, piece))(returned, x, gate, up, skip)
 
 
 def body(inputs, gate_values, filters, skip_weight, grad_out):
-    quarter = (lax.axis_index("seq") // 32).astype(jnp.int32).reshape(1)
-    every_filter = lax.all_gather(filters, "chan", axis=0, tiled=True)
+    quarter = (lax.axis_index("seq") >> 5).astype(jnp.int32).reshape(1)
+    rings = [[RING * plane + z for z in range(RING)] for plane in range(PLANES)]
+    planes = [[RING * plane + z for plane in range(PLANES)] for z in range(RING)]
+    every_filter = lax.all_gather(filters, "chan", axis=0)
     leaving = source(inputs, gate_values, grad_out, every_filter)
-    arrived = lax.all_to_all(leaving, "seq", split_axis=1, concat_axis=1, tiled=True)
+    ring = lax.all_to_all(
+        leaving, "seq", split_axis=0, concat_axis=0, tiled=True, axis_index_groups=rings
+    )
+    arrived = lax.all_to_all(
+        spread(ring), "seq", split_axis=0, concat_axis=0, tiled=True, axis_index_groups=planes
+    )
     results = middle(arrived, quarter)
-    returned = lax.all_to_all(results, "seq", split_axis=1, concat_axis=1, tiled=True)
-    grad_input, grad_gate, taps = final(
+    returned = lax.all_to_all(results, "seq", split_axis=0, concat_axis=0, tiled=True)
+    taps = final_taps(returned)
+    grad_filter = lax.psum_scatter(taps, "chan", scatter_dimension=0, tiled=True)
+    grad_input, grad_gate = final(
         returned, inputs, gate_values, grad_out, skip_weight[:, None]
     )
-    grad_filter = lax.psum_scatter(taps, "chan", scatter_dimension=0, tiled=True)
     return (grad_input, grad_gate, grad_filter)
 
 

time: 109 us -> 100 us (0.917)
  waiting for transfers between devices: 46 us -> 22.1 us
  blocking collectives: 20.6 us -> 43.7 us
  starting transfers between devices: 25.9 us -> 17 us
  Pallas kernels: 7.7 us -> 11.9 us
  local copies, waits for them, and re-layouts: 7.29 us -> 3.83 us
    all_to_all x2, waiting for transfers between devices: 46 us -> 22.1 us  [the longest x1 13.8 us: body(): lax.all_to_all(results, 'seq', split_axis=0, concat_axis=0, tiled=True)]
    all_to_all x0 -> x1, blocking collectives: none -> 22.5 us  [body(): lax.all_to_all(leaving, 'seq', split_axis=0, concat_axis=0, tiled=True, a...]
    all_to_all x2, starting transfers between devices: 25.9 us -> 17 us  [the longest x1 10.6 us: body(): lax.all_to_all(results, 'seq', split_axis=0, concat_axis=0, tiled=True)]
    pallas_call x3 -> x5, Pallas kernels: 7.7 us -> 11.9 us  [the longest x1 4.86 us: middle(): pl.pallas_call(middle_kernel, out_shape=jax.ShapeDtypeStruct((BLOCKS, 2,...]
    pallas_call x2 -> x0, local copies, waits for them, and re-layouts: 2.77 us -> none  [the longest x1 2.02 us: source(): pl.pallas_call(source_kernel, out_shape=jax.ShapeDtypeStruct((6, BLOCKS,...]
    unnamed x5 -> x6, local copies, waits for them, and re-layouts: 3.11 us -> 3.15 us
where the time goes in v1:
time: 100 us; the launch traced here: 99.9 us
  blocking collectives  43.7 us (44%)
  waiting for transfers between devices  22.1 us (22%)
  starting transfers between devices  17 us (17%)
  Pallas kernels  11.9 us (12%)
  local copies, waits for them, and re-layouts  3.83 us (4%)
  between operations  1.32 us (1%)
    all_to_all x1, blocking collectives, body(): lax.all_to_all(leaving, 'seq', split_axis=0, concat_axis=0, tiled=True, a...  22.5 us
    all_to_all x1, waiting for transfers between devices, body(): lax.all_to_all(results, 'seq', split_axis=0, concat_axis=0, tiled=True)  13.8 us
    all_gather x1, blocking collectives, body(): every_filter = lax.all_gather(filters, 'chan', axis=0)  12.5 us
    all_to_all x1, starting transfers between devices, body(): lax.all_to_all(results, 'seq', split_axis=0, concat_axis=0, tiled=True)  10.6 us
    unnamed x1, blocking collectives  8.72 us
    all_to_all x1, waiting for transfers between devices, body(): lax.all_to_all(spread(ring), 'seq', split_axis=0, concat_axis=0, tiled=Tr...  8.4 us
    all_to_all x1, starting transfers between devices, body(): lax.all_to_all(spread(ring), 'seq', split_axis=0, concat_axis=0, tiled=Tr...  6.36 us
    pallas_call x1, Pallas kernels, middle(): pl.pallas_call(middle_kernel, out_shape=jax.ShapeDtypeStruct((BLOCKS, 2,...  4.86 us
  transfers between devices with their start and end apart: 2, of which 2 were waited for; matrix products, arithmetic and copies ran while one was open for 2% of the time, Pallas kernels for 0%

profile of v1, /device:TPU:1, one launch (start us, length us, event | category | flops | bytes accessed | tf_op | source)
XLA Modules:
  0.0 99.9 jit_solution(269864794110373817)
XLA Ops:
  0.6 12.5 %all-gather.1.filter_ref = f32[4,2,256]{2,1,0:T(2,128)} all-gather(f32[1,2,256]{2,1,0:T(2,128)} %bitcast.4), channel_id=2, replica_groups=mesh['seq'=128,'chan'=4] {'chan'}, dimensions={0}, use_global_device_ids=true | all-gather | bytes 10240 | tf_op jit(solution)/shard_map/all_gather | solution.py:247
  13.1 1.5 %shard_map.76 = f32[16,16,128]{2,1,0:T(8,128)} custom-call(bf16[32,256]{1,0:T(8,128)(2,1)} %x_ref.3, bf16[32,256]{1,0:T(8,128)(2,1)} %gate_ref.3, bf16[32,256]{1,0:T(8,128)(2,1)} %up_ref.3, f32[4,2,256]{2,1,0:T(2,128)} %all-gather.1.filter_ref), custom_call_target="tpu_custom_call" | custom-call | tf_op jit(solution)/shard_map/pallas_call | solution.py:172
  14.6 22.5 %all_to_all.15.in_ref = f32[16,16,128]{2,1,0:T(8,128)} all-to-all(f32[16,16,128]{2,1,0:T(8,128)} %shard_map.76), channel_id=1, replica_groups={{0,4,8,12,16,20,24,28,32,36,40,44,48,52,56,60},{64,68,72,76,80,84,88,92..., dimensions={0} | all-to-all | bytes 262144 | tf_op jit(solution)/shard_map/all_to_all | solution.py:249
  37.1 1.7 %shard_map.77 = f32[8,6,16,128]{3,2,1,0:T(8,128)} custom-call(f32[16,16,128]{2,1,0:T(8,128)} %all_to_all.15.in_ref), custom_call_target="tpu_custom_call" | custom-call | tf_op jit(solution)/shard_map/pallas_call | solution.py:188
  38.8 6.4 %all-to-all-start.1 = ((f32[8,6,16,128]{3,2,1,0:T(8,128)}), f32[8,6,16,128]{3,2,1,0:T(8,128)S(1)}, u32[]{:S(2)}, u32[]{:S(2)}) async-start(f32[8,6,16,128]{3,2,1,0:T(8,128)} %shard_map.77), calls=%async_computation.1 | async-start | bytes 786432 | tf_op jit(solution)/shard_map/all_to_all | solution.py:252
  45.1 8.4 %all-to-all-done.1.a_ref = f32[8,6,16,128]{3,2,1,0:T(8,128)S(1)} async-done(((f32[8,6,16,128]{3,2,1,0:T(8,128)}), f32[8,6,16,128]{3,2,1,0:T(8,128)S(1)}, u32[]{:S(2)}, u32[]{:S(2)}) %all-to-all-start.1) | async-done | bytes 393248 | tf_op jit(solution)/shard_map/all_to_all | solution.py:252
  53.5 4.9 %shard_map.78 = f32[128,2,128]{2,1,0:T(2,128)} custom-call(s32[1]{0:T(128)} %bitcast.r_ref, f32[8,6,16,128]{3,2,1,0:T(8,128)S(1)} %all-to-all-done.1.a_ref), custom_call_target="tpu_custom_call" | custom-call | tf_op jit(solution)/shard_map/pallas_call | solution.py:138
  58.4 10.6 %all-to-all-start.2 = ((f32[128,2,128]{2,1,0:T(2,128)}), f32[128,2,128]{2,1,0:T(2,128)S(1)}, u32[]{:S(2)}, u32[]{:S(2)}) async-start(f32[128,2,128]{2,1,0:T(2,128)} %shard_map.78), calls=%async_computation.2 | async-start | bytes 262144 | tf_op jit(solution)/shard_map/all_to_all | solution.py:256
  69.0 0.0 copy-start.1
  69.0 0.6 copy-done.1
  69.7 0.7 copy.9.skip_ref
  70.4 1.3 %dynamic-slice = u32[1]{0:T(128)} dynamic-slice(u32[512]{0:T(512)} %constant.11, u32[]{:T(128)S(6)} %add.3), dynamic_slice_sizes={1} | dynamic-slice | bytes 12
  72.3 13.8 %all-to-all-done.2.b_ref = f32[128,2,128]{2,1,0:T(2,128)S(1)} async-done(((f32[128,2,128]{2,1,0:T(2,128)}), f32[128,2,128]{2,1,0:T(2,128)S(1)}, u32[]{:S(2)}, u32[]{:S(2)}) %all-to-all-start.2) | async-done | bytes 131104 | tf_op jit(solution)/shard_map/all_to_all | solution.py:256
  86.0 0.0 copy-start
  86.0 0.7 copy-done
  86.7 1.8 %shard_map.80 = f32[8,256]{1,0:T(8,128)} custom-call(f32[128,2,128]{2,1,0:T(2,128)} %copy-done), custom_call_target="tpu_custom_call" | custom-call | tf_op jit(solution)/shard_map/pallas_call | solution.py:220
  88.5 8.7 %all-reduce = f32[8,256]{1,0:T(8,128)S(1)} all-reduce(f32[8,256]{1,0:T(8,128)} %shard_map.80), channel_id=3, replica_groups=mesh['seq'=128,'chan'=4] {'chan'}, use_global_device_ids=true, to_apply=%region_0.0.clone | all-reduce | flops 2048 | bytes 16384
  97.2 0.6 constant_dynamic-slice_fusion
  97.8 2.1 %shard_map.79 = (bf16[32,256]{1,0:T(8,128)(2,1)}, bf16[32,256]{1,0:T(8,128)(2,1)}) custom-call(f32[128,2,128]{2,1,0:T(2,128)} %copy-done, bf16[32,256]{1,0:T(8,128)(2,1)} %x_ref.3, bf16[32,256]{1,0:T(8,128)(2,1)} %gate_ref.3, bf16[32,256]{1,0:T(8,128)(2,1)} %up_ref.3, f32[32,1]{1,0:T(8,128)} %copy.9.skip_ref), custom_call_target="tpu_custom_call" | custom-call | tf_op jit(solution)/shard_map/pallas_call | solution.py:240
Async XLA Ops:
  38.8 14.8 %all-to-all-start.1 = ((f32[8,6,16,128]{3,2,1,0:T(8,128)}), f32[8,6,16,128]{3,2,1,0:T(8,128)S(1)}, u32[]{:S(2)}, u32[]{:S(2)}) async-start(f32[8,6,16,128]{3,2,1,0:T(8,128)} %shard_map.77), calls=%async_computation.1 | async-start | bytes 786432 | tf_op jit(solution)/shard_map/all_to_all | solution.py:252
  58.4 27.6 %all-to-all-start.2 = ((f32[128,2,128]{2,1,0:T(2,128)}), f32[128,2,128]{2,1,0:T(2,128)S(1)}, u32[]{:S(2)}, u32[]{:S(2)}) async-start(f32[128,2,128]{2,1,0:T(2,128)} %shard_map.78), calls=%async_computation.2 | async-start | bytes 262144 | tf_op jit(solution)/shard_map/all_to_all | solution.py:256
  69.0 0.7 copy-start.1
  86.0 0.7 copy-start

commit v2 on v1

--- a/solution.py
+++ b/solution.py
@@ -51,7 +51,7 @@
     r = r_ref[0]
 
     def signal(first):
-        halves = [a_ref[:, first + half].reshape(BLOCKS, 128) for half in range(2)]
+        halves = [a_ref[pl.ds(first + half, BLOCKS, stride=6), :] for half in range(2)]
         return jnp.concatenate(halves, axis=1)
 
     x, g, h = signal(0), signal(2), signal(4)
@@ -130,14 +130,14 @@
             total = total + jnp.dot(high, pick, preferred_element_type=F32)
             total = total + jnp.dot(low, pick, preferred_element_type=F32)
         totals[page] = total
-    out_ref[:, 0] = totals[0]
-    out_ref[:, 1] = totals[1]
+    out_ref[pl.ds(0, BLOCKS, stride=2), :] = totals[0]
+    out_ref[pl.ds(1, BLOCKS, stride=2), :] = totals[1]
 
 
 def middle(arrived, r):
     return pl.pallas_call(
         middle_kernel,
-        out_shape=jax.ShapeDtypeStruct((BLOCKS, 2, 128), F32),
+        out_shape=jax.ShapeDtypeStruct((2 * BLOCKS, 128), F32),
         in_specs=[
             pl.BlockSpec(memory_space=pltpu.SMEM),
             pl.BlockSpec(memory_space=pltpu.VMEM),
@@ -152,43 +152,29 @@
     )(r, arrived)
 
 
-RING = 16
-PLANES = 8
+VMEM = pl.BlockSpec(memory_space=pltpu.VMEM)
 
 
 def source_kernel(x_ref, gate_ref, up_ref, filter_ref, out_ref):
     x = x_ref[...].astype(F32)
     mixed = up_ref[...].astype(F32) * gate_ref[...].astype(F32)
-    filters = jnp.concatenate([filter_ref[i] for i in range(4)] * 2, axis=0)
+    filters = jnp.concatenate([filter_ref[i] for i in range(4)] * 4, axis=0)
     line = 0
-    for value in (x[:RING], x[RING:], mixed[:RING], mixed[RING:], filters):
+    for value in (x, mixed, filters):
         for half in range(2):
-            out_ref[:, line] = value[:, 128 * half : 128 * half + 128]
+            part = value[:, 128 * half : 128 * half + 128]
+            part = jnp.concatenate([part] * QUARTERS, axis=0)
+            out_ref[pl.ds(line, BLOCKS, stride=6), :] = part
             line += 1
-    out_ref[:, line:] = jnp.zeros((RING, 16 - line, 128), F32)
 
 
 def source(x, gate, up, filters):
     return pl.pallas_call(
         source_kernel,
-        out_shape=jax.ShapeDtypeStruct((RING, 16, 128), F32),
+        out_shape=jax.ShapeDtypeStruct((6 * BLOCKS, 128), F32),
+        in_specs=[VMEM] * 4,
+        out_specs=VMEM,
     )(x, gate, up, filters)
-
-
-def spread_kernel(in_ref, out_ref):
-    lines = [in_ref[:, line] for line in range(10)]
-    for plane in range(PLANES):
-        member = plane % 2
-        chosen = (2 * member, 2 * member + 1, 4 + 2 * member, 5 + 2 * member, 8, 9)
-        for place, line in enumerate(chosen):
-            out_ref[plane, place] = lines[line]
-
-
-def spread(ring):
-    return pl.pallas_call(
-        spread_kernel,
-        out_shape=jax.ShapeDtypeStruct((PLANES, 6, RING, 128), F32),
-    )(ring)
 
 
 def exact_dot(value, pick):
@@ -208,24 +194,44 @@
     return (place == target).astype(BF16)
 
 
+def sums_kernel(b_ref, out_ref):
+    for quarter in range(QUARTERS):
+        rows = b_ref[pl.ds(64 * quarter + 1, 32, stride=2), :]
+        total = rows.reshape(4, 8, 128).sum(axis=0)
+        for owner in range(4):
+            out_ref[owner, 2 * quarter : 2 * quarter + 2] = total[2 * owner : 2 * owner + 2]
+
+
+def sums(returned):
+    return pl.pallas_call(
+        sums_kernel,
+        out_shape=jax.ShapeDtypeStruct((4, 8, 128), F32),
+        in_specs=[VMEM],
+        out_specs=VMEM,
+    )(returned)
+
+
 def taps_kernel(b_ref, gf_ref):
-    taps = jnp.zeros((8, BLOCK), F32)
+    taps = jnp.zeros((2, BLOCK), F32)
+    cross = (b_ref[0] + b_ref[1]) + (b_ref[2] + b_ref[3])
     for quarter in range(QUARTERS):
-        cross = b_ref[32 * quarter : 32 * quarter + 32, 1].reshape(4, 8, 128).sum(axis=0)
-        taps = taps + exact_dot(cross, quarter_pick(quarter, BLOCK))
+        taps = taps + exact_dot(cross[2 * quarter : 2 * quarter + 2], quarter_pick(quarter, BLOCK))
     gf_ref[...] = taps * (1.0 / math.sqrt(BLOCKS * BLOCK))
 
 
-def final_taps(returned):
-    return pl.pallas_call(
-        taps_kernel, out_shape=jax.ShapeDtypeStruct((8, BLOCK), F32)
-    )(returned)
+def final_taps(parts):
+    return pl.pallas_call(
+        taps_kernel,
+        out_shape=jax.ShapeDtypeStruct((2, BLOCK), F32),
+        in_specs=[VMEM],
+        out_specs=VMEM,
+    )(parts)
 
 
 def final_kernel(b_ref, x_ref, gate_ref, up_ref, skip_ref, gi_ref, gg_ref):
     both = jnp.zeros((32, 2 * BLOCK), F32)
     for quarter in range(QUARTERS):
-        rows = b_ref[32 * quarter : 32 * quarter + 32, 0]
+        rows = b_ref[pl.ds(64 * quarter, 32, stride=2), :]
         both = both + exact_dot(rows, quarter_pick(quarter, 2 * BLOCK))
     x = x_ref[...].astype(F32)
     up = up_ref[...].astype(F32)
@@ -237,29 +243,31 @@
 
 def final(returned, x, gate, up, skip):
     piece = jax.ShapeDtypeStruct((32, BLOCK), BF16)
-    return pl.pallas_call(final_kernel, out_shape=(piece, piece))(returned, x, gate, up, skip)
+    return pl.pallas_call(
+        final_kernel,
+        out_shape=(piece, piece),
+        in_specs=[VMEM] * 5,
+        out_specs=[VMEM] * 2,
+    )(returned, x, gate, up, skip)
+
+
+def exchange(rows):
+    flat = rows.reshape(BLOCKS, 1, -1)
+    flat = lax.all_to_all(flat, "seq", split_axis=0, concat_axis=0, tiled=True)
+    return flat.reshape(rows.shape)
 
 
 def body(inputs, gate_values, filters, skip_weight, grad_out):
     quarter = (lax.axis_index("seq") >> 5).astype(jnp.int32).reshape(1)
-    rings = [[RING * plane + z for z in range(RING)] for plane in range(PLANES)]
-    planes = [[RING * plane + z for plane in range(PLANES)] for z in range(RING)]
     every_filter = lax.all_gather(filters, "chan", axis=0)
     leaving = source(inputs, gate_values, grad_out, every_filter)
-    ring = lax.all_to_all(
-        leaving, "seq", split_axis=0, concat_axis=0, tiled=True, axis_index_groups=rings
-    )
-    arrived = lax.all_to_all(
-        spread(ring), "seq", split_axis=0, concat_axis=0, tiled=True, axis_index_groups=planes
-    )
-    results = middle(arrived, quarter)
-    returned = lax.all_to_all(results, "seq", split_axis=0, concat_axis=0, tiled=True)
-    taps = final_taps(returned)
-    grad_filter = lax.psum_scatter(taps, "chan", scatter_dimension=0, tiled=True)
+    results = middle(exchange(leaving), quarter)
+    returned = exchange(results)
+    shares = lax.all_to_all(sums(returned), "chan", split_axis=0, concat_axis=0, tiled=True)
     grad_input, grad_gate = final(
         returned, inputs, gate_values, grad_out, skip_weight[:, None]
     )
-    return (grad_input, grad_gate, grad_filter)
+    return (grad_input, grad_gate, final_taps(shares))
 
 
 def solution(mesh):

time: 100 us -> 103 us (1.030)
  starting transfers between devices: 17 us -> 23.9 us
  blocking collectives: 43.7 us -> 37.2 us
  waiting for transfers between devices: 22.1 us -> 28 us
  local copies, waits for them, and re-layouts: 3.83 us -> 1.94 us
  Pallas kernels: 11.9 us -> 10.7 us
    unnamed x1 -> x0, blocking collectives: 8.72 us -> none
    all_to_all x2, starting transfers between devices: 17 us -> 23.9 us  [the longest x1 17.2 us: exchange(): flat = lax.all_to_all(flat, 'seq', split_axis=0, concat_axis=0, tiled=True)]
    all_to_all x2, waiting for transfers between devices: 22.1 us -> 28 us  [the longest x1 28 us: exchange(): flat = lax.all_to_all(flat, 'seq', split_axis=0, concat_axis=0, tiled=True)]
    all_to_all x1, blocking collectives: 22.5 us -> 24.7 us  [exchange(): flat = lax.all_to_all(flat, 'seq', split_axis=0, concat_axis=0, tiled=True)]
    unnamed x6 -> x4, local copies, waits for them, and re-layouts: 3.15 us -> 1.25 us
    pallas_call x5, Pallas kernels: 11.9 us -> 10.7 us  [the longest x1 4.19 us: middle(): pl.pallas_call(middle_kernel, out_shape=jax.ShapeDtypeStruct((2 * BLOCKS,...]
  transfers between devices with their start and end apart: 2 -> 2, of which waited for: 2 -> 1; matrix products, arithmetic and copies ran while one was open for 2% -> 1% of each run, Pallas kernels for 0% -> 2%
where the time goes in v2:
time: 103 us; the launch traced here: 102 us
  blocking collectives  37.2 us (36%)
  waiting for transfers between devices  28 us (27%)
  starting transfers between devices  23.9 us (23%)
  Pallas kernels  10.7 us (10%)
  local copies, waits for them, and re-layouts  1.94 us (2%)
    all_to_all x1, waiting for transfers between devices, exchange(): flat = lax.all_to_all(flat, 'seq', split_axis=0, concat_axis=0, tiled=True)  28 us
    all_to_all x1, blocking collectives, exchange(): flat = lax.all_to_all(flat, 'seq', split_axis=0, concat_axis=0, tiled=True)  24.7 us
    all_to_all x1, starting transfers between devices, exchange(): flat = lax.all_to_all(flat, 'seq', split_axis=0, concat_axis=0, tiled=True)  17.2 us
    all_gather x1, blocking collectives, body(): every_filter = lax.all_gather(filters, 'chan', axis=0)  12.5 us
    all_to_all x1, starting transfers between devices, body(): lax.all_to_all(sums(returned), 'chan', split_axis=0, concat_axis=0, tiled...  6.69 us
    pallas_call x1, Pallas kernels, middle(): pl.pallas_call(middle_kernel, out_shape=jax.ShapeDtypeStruct((2 * BLOCKS,...  4.19 us
  transfers between devices with their start and end apart: 2, of which 1 were waited for; matrix products, arithmetic and copies ran while one was open for 1% of the time, Pallas kernels for 2%

profile of v2, /device:TPU:1, one launch (start us, length us, event | category | flops | bytes accessed | tf_op | source)
XLA Modules:
  0.0 102.4 jit_solution(2595365078906364953)
XLA Ops:
  0.6 12.5 %all-gather.1.filter_ref = f32[4,2,256]{2,1,0:T(2,128)} all-gather(f32[1,2,256]{2,1,0:T(2,128)} %bitcast.12), channel_id=2, replica_groups=mesh['seq'=128,'chan'=4] {'chan'}, dimensions={0}, use_global_device_ids=true | all-gather | bytes 10240 | tf_op jit(solution)/shard_map/all_gather | solution.py:262
  13.1 1.5 %shard_map.76 = f32[768,128]{1,0:T(8,128)} custom-call(bf16[32,256]{1,0:T(8,128)(2,1)} %x_ref.3, bf16[32,256]{1,0:T(8,128)(2,1)} %gate_ref.3, bf16[32,256]{1,0:T(8,128)(2,1)} %up_ref.3, f32[4,2,256]{2,1,0:T(2,128)} %all-gather.1.filter_ref), custom_call_target="tpu_custom_call" | custom-call | tf_op jit(solution)/shard_map/pallas_call | solution.py:172
  14.7 17.2 %all-to-all-start = ((f32[128,1,768]{2,1,0:T(1,128)}), f32[128,1,768]{2,1,0:T(1,128)S(1)}, u32[]{:S(2)}, u32[]{:S(2)}) async-start(f32[128,1,768]{2,1,0:T(1,128)} %bitcast.9), calls=%async_computation | async-start | bytes 786432 | tf_op jit(solution)/shard_map/all_to_all | solution.py:256
  31.8 28.0 %all-to-all-done = f32[128,1,768]{2,1,0:T(1,128)S(1)} async-done(((f32[128,1,768]{2,1,0:T(1,128)}), f32[128,1,768]{2,1,0:T(1,128)S(1)}, u32[]{:S(2)}, u32[]{:S(2)}) %all-to-all-start) | async-done | bytes 393248 | tf_op jit(solution)/shard_map/all_to_all | solution.py:256
  59.9 4.2 %shard_map.77 = f32[256,128]{1,0:T(8,128)S(1)} custom-call(s32[1]{0:T(128)} %bitcast.r_ref, f32[768,128]{1,0:T(8,128)S(1)} %bitcast.7), custom_call_target="tpu_custom_call" | custom-call | tf_op jit(solution)/shard_map/pallas_call | solution.py:138
  64.1 24.7 %all_to_all.15 = f32[128,1,256]{2,1,0:T(1,128)} all-to-all(f32[128,1,256]{2,1,0:T(1,128)S(1)} %bitcast.8), channel_id=1, replica_groups=mesh['seq'=128,'chan'=4] {'seq'}, dimensions={0} | all-to-all | bytes 262144 | tf_op jit(solution)/shard_map/all_to_all | solution.py:256
  88.8 1.5 %shard_map.79 = f32[4,8,128]{2,1,0:T(8,128)} custom-call(f32[256,128]{1,0:T(8,128)} %bitcast.10), custom_call_target="tpu_custom_call" | custom-call | tf_op jit(solution)/shard_map/pallas_call | solution.py:206
  90.3 6.7 %all-to-all-start.2 = ((f32[4,8,128]{2,1,0:T(8,128)}), f32[4,8,128]{2,1,0:T(8,128)S(1)}, u32[]{:S(2)}, u32[]{:S(2)}) async-start(f32[4,8,128]{2,1,0:T(8,128)} %shard_map.79), calls=%async_computation.2 | async-start | bytes 32768 | tf_op jit(solution)/shard_map/all_to_all | solution.py:266
  97.0 0.0 copy-start.1
  97.0 0.7 copy-done.1
  97.6 0.7 copy.11.skip_ref
  98.3 1.9 %shard_map.78 = (bf16[32,256]{1,0:T(8,128)(2,1)}, bf16[32,256]{1,0:T(8,128)(2,1)}) custom-call(f32[256,128]{1,0:T(8,128)} %bitcast.11, bf16[32,256]{1,0:T(8,128)(2,1)} %x_ref.3, bf16[32,256]{1,0:T(8,128)(2,1)} %gate_ref.3, bf16[32,256]{1,0:T(8,128)(2,1)} %up_ref.3, f32[32,1]{1,0:T(8,128)} %copy.11.skip_ref), custom_call_target="tpu_custom_call" | custom-call | tf_op jit(solution)/shard_map/pallas_call | solution.py:246
  100.2 0.0 all-to-all-done.2.b_ref
  100.2 0.0 copy-start
  100.2 0.6 copy-done
  100.8 1.6 %shard_map.80 = f32[2,256]{1,0:T(2,128)} custom-call(f32[4,8,128]{2,1,0:T(8,128)} %copy-done), custom_call_target="tpu_custom_call" | custom-call | tf_op jit(solution)/shard_map/pallas_call | solution.py:223
Async XLA Ops:
  14.7 45.2 %all-to-all-start = ((f32[128,1,768]{2,1,0:T(1,128)}), f32[128,1,768]{2,1,0:T(1,128)S(1)}, u32[]{:S(2)}, u32[]{:S(2)}) async-start(f32[128,1,768]{2,1,0:T(1,128)} %bitcast.9), calls=%async_computation | async-start | bytes 786432 | tf_op jit(solution)/shard_map/all_to_all | solution.py:256
  90.3 10.0 %all-to-all-start.2 = ((f32[4,8,128]{2,1,0:T(8,128)}), f32[4,8,128]{2,1,0:T(8,128)S(1)}, u32[]{:S(2)}, u32[]{:S(2)}) async-start(f32[4,8,128]{2,1,0:T(8,128)} %shard_map.79), calls=%async_computation.2 | async-start | bytes 32768 | tf_op jit(solution)/shard_map/all_to_all | solution.py:266
  97.0 0.7 copy-start.1
  100.2 0.6 copy-start

commit v3 on v2

--- a/solution.py
+++ b/solution.py
@@ -51,7 +51,7 @@
     r = r_ref[0]
 
     def signal(first):
-        halves = [a_ref[pl.ds(first + half, BLOCKS, stride=6), :] for half in range(2)]
+        halves = [a_ref[:, first + half].reshape(BLOCKS, 128) for half in range(2)]
         return jnp.concatenate(halves, axis=1)
 
     x, g, h = signal(0), signal(2), signal(4)
@@ -148,33 +148,55 @@
             pltpu.VMEM((4, PARTS, BLOCKS, BLOCK), BF16),
             pltpu.VMEM((3, PARTS, BLOCKS, BLOCK), F32),
         ],
-        compiler_params=pltpu.CompilerParams(vmem_limit_bytes=48 * 1024 * 1024),
+        compiler_params=pltpu.CompilerParams(vmem_limit_bytes=16 * 1024 * 1024),
     )(r, arrived)
 
 
 VMEM = pl.BlockSpec(memory_space=pltpu.VMEM)
+SMALL = pltpu.CompilerParams(vmem_limit_bytes=4 * 1024 * 1024)
+RING = 16
+PLANES = 8
 
 
 def source_kernel(x_ref, gate_ref, up_ref, filter_ref, out_ref):
     x = x_ref[...].astype(F32)
     mixed = up_ref[...].astype(F32) * gate_ref[...].astype(F32)
-    filters = jnp.concatenate([filter_ref[i] for i in range(4)] * 4, axis=0)
+    filters = jnp.concatenate([filter_ref[i] for i in range(4)] * 2, axis=0)
     line = 0
-    for value in (x, mixed, filters):
+    for value in (x[:RING], x[RING:], mixed[:RING], mixed[RING:], filters):
         for half in range(2):
-            part = value[:, 128 * half : 128 * half + 128]
-            part = jnp.concatenate([part] * QUARTERS, axis=0)
-            out_ref[pl.ds(line, BLOCKS, stride=6), :] = part
+            out_ref[:, line] = value[:, 128 * half : 128 * half + 128]
             line += 1
+    out_ref[:, line:] = jnp.zeros((RING, 16 - line, 128), F32)
 
 
 def source(x, gate, up, filters):
     return pl.pallas_call(
         source_kernel,
-        out_shape=jax.ShapeDtypeStruct((6 * BLOCKS, 128), F32),
+        out_shape=jax.ShapeDtypeStruct((RING, 16, 128), F32),
         in_specs=[VMEM] * 4,
         out_specs=VMEM,
+        compiler_params=SMALL,
     )(x, gate, up, filters)
+
+
+def spread_kernel(in_ref, out_ref):
+    lines = [in_ref[:, line] for line in range(10)]
+    for plane in range(PLANES):
+        member = plane % 2
+        chosen = (2 * member, 2 * member + 1, 4 + 2 * member, 5 + 2 * member, 8, 9)
+        for place, line in enumerate(chosen):
+            out_ref[plane, place] = lines[line]
+
+
+def spread(ring):
+    return pl.pallas_call(
+        spread_kernel,
+        out_shape=jax.ShapeDtypeStruct((PLANES, 6, RING, 128), F32),
+        in_specs=[VMEM],
+        out_specs=VMEM,
+        compiler_params=SMALL,
+    )(ring)
 
 
 def exact_dot(value, pick):
@@ -208,6 +230,7 @@
         out_shape=jax.ShapeDtypeStruct((4, 8, 128), F32),
         in_specs=[VMEM],
         out_specs=VMEM,
+        compiler_params=SMALL,
     )(returned)
 
 
@@ -225,6 +248,7 @@
         out_shape=jax.ShapeDtypeStruct((2, BLOCK), F32),
         in_specs=[VMEM],
         out_specs=VMEM,
+        compiler_params=SMALL,
     )(parts)
 
 
@@ -248,6 +272,7 @@
         out_shape=(piece, piece),
         in_specs=[VMEM] * 5,
         out_specs=[VMEM] * 2,
+        compiler_params=SMALL,
     )(returned, x, gate, up, skip)
 
 
@@ -260,8 +285,16 @@
 def body(inputs, gate_values, filters, skip_weight, grad_out):
     quarter = (lax.axis_index("seq") >> 5).astype(jnp.int32).reshape(1)
     every_filter = lax.all_gather(filters, "chan", axis=0)
+    rings = [[RING * plane + z for z in range(RING)] for plane in range(PLANES)]
+    planes = [[RING * plane + z for plane in range(PLANES)] for z in range(RING)]
     leaving = source(inputs, gate_values, grad_out, every_filter)
-    results = middle(exchange(leaving), quarter)
+    ring = lax.all_to_all(
+        leaving, "seq", split_axis=0, concat_axis=0, tiled=True, axis_index_groups=rings
+    )
+    arrived = lax.all_to_all(
+        spread(ring), "seq", split_axis=0, concat_axis=0, tiled=True, axis_index_groups=planes
+    )
+    results = middle(arrived, quarter)
     returned = exchange(results)
     shares = lax.all_to_all(sums(returned), "chan", split_axis=0, concat_axis=0, tiled=True)
     grad_input, grad_gate = final(

time: 103 us -> 95.9 us (0.931)
  blocking collectives: 37.2 us -> 60.9 us
  waiting for transfers between devices: 28 us -> 9.84 us
  starting transfers between devices: 23.9 us -> 13.5 us
  Pallas kernels: 10.7 us -> 7.46 us
    all_to_all x0 -> x1, blocking collectives: none -> 21.5 us  [body(): lax.all_to_all(leaving, 'seq', split_axis=0, concat_axis=0, tiled=True, a...]
    all_to_all x1, waiting for transfers between devices: 28 us -> 8.4 us  [body(): lax.all_to_all(spread(ring), 'seq', split_axis=0, concat_axis=0, tiled=Tr...]
    all_to_all x1, starting transfers between devices: 17.2 us -> 6.65 us  [body(): lax.all_to_all(spread(ring), 'seq', split_axis=0, concat_axis=0, tiled=Tr...]
    all_to_all x1, blocking collectives: 24.7 us -> 27.4 us  [exchange(): flat = lax.all_to_all(flat, 'seq', split_axis=0, concat_axis=0, tiled=True)]
    unnamed x4 -> x14, local copies, waits for them, and re-layouts: 1.25 us -> 2.78 us
    all_to_all x1, waiting for transfers between devices: 0.01 us -> 1.44 us  [body(): lax.all_to_all(sums(returned), 'chan', split_axis=0, concat_axis=0, tiled...]
  transfers between devices with their start and end apart: 2 -> 2, of which waited for: 1 -> 2; matrix products, arithmetic and copies ran while one was open for 1% -> 0% of each run, Pallas kernels for 2% -> 1%
where the time goes in v3:
time: 95.9 us; the launch traced here: 95.2 us
  blocking collectives  60.9 us (64%)
  starting transfers between devices  13.5 us (14%)
  waiting for transfers between devices  9.84 us (10%)
  Pallas kernels  7.46 us (8%)
  local copies, waits for them, and re-layouts  2.87 us (3%)
    all_to_all x1, blocking collectives, exchange(): flat = lax.all_to_all(flat, 'seq', split_axis=0, concat_axis=0, tiled=True)  27.4 us
    all_to_all x1, blocking collectives, body(): lax.all_to_all(leaving, 'seq', split_axis=0, concat_axis=0, tiled=True, a...  21.5 us
    all_gather x1, blocking collectives, body(): every_filter = lax.all_gather(filters, 'chan', axis=0)  12 us
    all_to_all x1, waiting for transfers between devices, body(): lax.all_to_all(spread(ring), 'seq', split_axis=0, concat_axis=0, tiled=Tr...  8.4 us
    all_to_all x1, starting transfers between devices, body(): lax.all_to_all(sums(returned), 'chan', split_axis=0, concat_axis=0, tiled...  6.87 us
    all_to_all x1, starting transfers between devices, body(): lax.all_to_all(spread(ring), 'seq', split_axis=0, concat_axis=0, tiled=Tr...  6.65 us
    pallas_call x1, Pallas kernels, middle(): pl.pallas_call(middle_kernel, out_shape=jax.ShapeDtypeStruct((2 * BLOCKS,...  4.19 us
    unnamed x14, local copies, waits for them, and re-layouts  2.78 us
  transfers between devices with their start and end apart: 2, of which 2 were waited for; matrix products, arithmetic and copies ran while one was open for 0% of the time, Pallas kernels for 1%

profile of v3, /device:TPU:1, one launch (start us, length us, event | category | flops | bytes accessed | tf_op | source)
XLA Modules:
  0.0 95.2 jit_solution(9136643383165553250)
XLA Ops:
  0.6 12.0 %all-gather.1.filter_ref = f32[4,2,256]{2,1,0:T(2,128)S(1)} all-gather(f32[1,2,256]{2,1,0:T(2,128)} %bitcast.8), channel_id=2, replica_groups=mesh['seq'=128,'chan'=4] {'chan'}, dimensions={0}, use_global_device_ids=true | all-gather | bytes 10240 | tf_op jit(solution)/shard_map/all_gather | solution.py:287
  12.6 0.0 copy-start
  12.6 0.7 copy-done
  13.3 0.0 copy-start.2
  13.3 0.7 copy-done.2
  14.0 0.0 copy-start.4
  14.0 0.7 copy-done.4
  14.8 0.1 shard_map.76
  14.8 21.5 %all_to_all.20.in_ref = f32[16,16,128]{2,1,0:T(8,128)S(1)} all-to-all(f32[16,16,128]{2,1,0:T(8,128)S(1)} %shard_map.76), channel_id=1, replica_groups={{0,4,8,12,16,20,24,28,32,36,40,44,48,52,56,60},{64,68,72,76,80,84,88,92..., dimensions={0} | all-to-all | bytes 262144 | tf_op jit(solution)/shard_map/all_to_all | solution.py:291
  36.3 0.8 shard_map.77
  37.1 6.7 %all-to-all-start.1 = ((f32[8,6,16,128]{3,2,1,0:T(8,128)}), f32[8,6,16,128]{3,2,1,0:T(8,128)S(1)}, u32[]{:S(2)}, u32[]{:S(2)}) async-start(f32[8,6,16,128]{3,2,1,0:T(8,128)} %shard_map.77), calls=%async_computation.1 | async-start | bytes 786432 | tf_op jit(solution)/shard_map/all_to_all | solution.py:294
  43.8 8.4 %all-to-all-done.1.a_ref = f32[8,6,16,128]{3,2,1,0:T(8,128)S(1)} async-done(((f32[8,6,16,128]{3,2,1,0:T(8,128)}), f32[8,6,16,128]{3,2,1,0:T(8,128)S(1)}, u32[]{:S(2)}, u32[]{:S(2)}) %all-to-all-start.1) | async-done | bytes 393248 | tf_op jit(solution)/shard_map/all_to_all | solution.py:294
  52.2 4.2 %shard_map.78 = f32[256,128]{1,0:T(8,128)S(1)} custom-call(s32[1]{0:T(128)} %bitcast.r_ref, f32[8,6,16,128]{3,2,1,0:T(8,128)S(1)} %all-to-all-done.1.a_ref), custom_call_target="tpu_custom_call" | custom-call | tf_op jit(solution)/shard_map/pallas_call | solution.py:138
  56.3 27.4 %all_to_all.21 = f32[128,1,256]{2,1,0:T(1,128)S(1)} all-to-all(f32[128,1,256]{2,1,0:T(1,128)S(1)} %bitcast.7), channel_id=1, replica_groups=mesh['seq'=128,'chan'=4] {'seq'}, dimensions={0} | all-to-all | bytes 262144 | tf_op jit(solution)/shard_map/all_to_all | solution.py:281
  83.8 0.6 shard_map.80
  84.4 0.0 copy-start.6
  84.4 0.0 copy-start.3
  84.4 0.0 copy-start.5
  84.4 6.9 %all-to-all-start.3 = ((f32[4,8,128]{2,1,0:T(8,128)}), f32[4,8,128]{2,1,0:T(8,128)S(1)}, u32[]{:S(2)}, u32[]{:S(2)}) async-start(f32[4,8,128]{2,1,0:T(8,128)} %shard_map.80), calls=%async_computation.3 | async-start | bytes 32768 | tf_op jit(solution)/shard_map/all_to_all | solution.py:299
  91.3 0.0 copy-start.1
  91.3 0.0 copy-done.6
  91.3 0.1 copy.10.skip_ref
  91.4 0.0 copy-done.3
  91.4 0.0 copy-done.5
  91.4 0.6 copy-done.1
  92.0 1.0 %shard_map.79 = (bf16[32,256]{1,0:T(8,128)(2,1)}, bf16[32,256]{1,0:T(8,128)(2,1)}) custom-call(f32[256,128]{1,0:T(8,128)S(1)} %bitcast.6, bf16[32,256]{1,0:T(8,128)(2,1)S(1)} %copy-done.1, bf16[32,256]{1,0:T(8,128)(2,1)S(1)} %copy-done.3, bf16[32,256]{1,0:T(8,128)(2,1)S(1)} %copy-done.5, f32[32,1]{1,0:T(8,128)S(1)} %copy.10.skip_ref), custom_call_target="tpu_custom_call" | custom-call | tf_op jit(solution)/shard_map/pallas_call | solution.py:270
  93.0 1.4 %all-to-all-done.3.b_ref = f32[4,8,128]{2,1,0:T(8,128)S(1)} async-done(((f32[4,8,128]{2,1,0:T(8,128)}), f32[4,8,128]{2,1,0:T(8,128)S(1)}, u32[]{:S(2)}, u32[]{:S(2)}) %all-to-all-start.3) | async-done | bytes 16416 | tf_op jit(solution)/shard_map/all_to_all | solution.py:299
  94.4 0.8 shard_map.81
Async XLA Ops:
  12.6 0.7 copy-start
  13.3 0.7 copy-start.2
  14.0 0.7 copy-start.4
  37.1 15.0 %all-to-all-start.1 = ((f32[8,6,16,128]{3,2,1,0:T(8,128)}), f32[8,6,16,128]{3,2,1,0:T(8,128)S(1)}, u32[]{:S(2)}, u32[]{:S(2)}) async-start(f32[8,6,16,128]{3,2,1,0:T(8,128)} %shard_map.77), calls=%async_computation.1 | async-start | bytes 786432 | tf_op jit(solution)/shard_map/all_to_all | solution.py:294
  84.4 6.9 %copy-start.6 = (f32[32]{0:T(128)S(1)}, f32[32]{0:T(128)}, u32[]{:S(2)}) copy-start(f32[32]{0:T(128)} %param.8) | copy-start | bytes 388
  84.4 7.0 %copy-start.3 = (bf16[32,256]{1,0:T(8,128)(2,1)S(1)}, bf16[32,256]{1,0:T(8,128)(2,1)}, u32[]{:S(2)}) copy-start(bf16[32,256]{1,0:T(8,128)(2,1)} %gate_ref.3) | copy-start | bytes 49156
  84.4 7.0 %copy-start.5 = (bf16[32,256]{1,0:T(8,128)(2,1)S(1)}, bf16[32,256]{1,0:T(8,128)(2,1)}, u32[]{:S(2)}) copy-start(bf16[32,256]{1,0:T(8,128)(2,1)} %up_ref.3) | copy-start | bytes 49156
  84.4 10.0 %all-to-all-start.3 = ((f32[4,8,128]{2,1,0:T(8,128)}), f32[4,8,128]{2,1,0:T(8,128)S(1)}, u32[]{:S(2)}, u32[]{:S(2)}) async-start(f32[4,8,128]{2,1,0:T(8,128)} %shard_map.80), calls=%async_computation.3 | async-start | bytes 32768 | tf_op jit(solution)/shard_map/all_to_all | solution.py:299
  91.3 0.7 copy-start.1

commit v4 on v2

--- a/solution.py
+++ b/solution.py
@@ -148,33 +148,33 @@
             pltpu.VMEM((4, PARTS, BLOCKS, BLOCK), BF16),
             pltpu.VMEM((3, PARTS, BLOCKS, BLOCK), F32),
         ],
-        compiler_params=pltpu.CompilerParams(vmem_limit_bytes=48 * 1024 * 1024),
+        compiler_params=pltpu.CompilerParams(vmem_limit_bytes=16 * 1024 * 1024),
     )(r, arrived)
 
 
 VMEM = pl.BlockSpec(memory_space=pltpu.VMEM)
-
-
-def source_kernel(x_ref, gate_ref, up_ref, filter_ref, out_ref):
-    x = x_ref[...].astype(F32)
-    mixed = up_ref[...].astype(F32) * gate_ref[...].astype(F32)
+SMALL = pltpu.CompilerParams(vmem_limit_bytes=4 * 1024 * 1024)
+MEMBERS = 32
+
+
+def source_kernel(signal_ref, filter_ref, out_ref):
     filters = jnp.concatenate([filter_ref[i] for i in range(4)] * 4, axis=0)
     line = 0
-    for value in (x, mixed, filters):
+    for value in (signal_ref[:MEMBERS], signal_ref[MEMBERS:], filters):
         for half in range(2):
             part = value[:, 128 * half : 128 * half + 128]
-            part = jnp.concatenate([part] * QUARTERS, axis=0)
-            out_ref[pl.ds(line, BLOCKS, stride=6), :] = part
+            out_ref[pl.ds(line, MEMBERS, stride=6), :] = part
             line += 1
 
 
-def source(x, gate, up, filters):
+def source(signals, filters):
     return pl.pallas_call(
         source_kernel,
-        out_shape=jax.ShapeDtypeStruct((6 * BLOCKS, 128), F32),
-        in_specs=[VMEM] * 4,
+        out_shape=jax.ShapeDtypeStruct((6 * MEMBERS, 128), F32),
+        in_specs=[VMEM] * 2,
         out_specs=VMEM,
-    )(x, gate, up, filters)
+        compiler_params=SMALL,
+    )(signals, filters)
 
 
 def exact_dot(value, pick):
@@ -208,6 +208,7 @@
         out_shape=jax.ShapeDtypeStruct((4, 8, 128), F32),
         in_specs=[VMEM],
         out_specs=VMEM,
+        compiler_params=SMALL,
     )(returned)
 
 
@@ -225,6 +226,7 @@
         out_shape=jax.ShapeDtypeStruct((2, BLOCK), F32),
         in_specs=[VMEM],
         out_specs=VMEM,
+        compiler_params=SMALL,
     )(parts)
 
 
@@ -248,21 +250,31 @@
         out_shape=(piece, piece),
         in_specs=[VMEM] * 5,
         out_specs=[VMEM] * 2,
+        compiler_params=SMALL,
     )(returned, x, gate, up, skip)
 
 
-def exchange(rows):
-    flat = rows.reshape(BLOCKS, 1, -1)
-    flat = lax.all_to_all(flat, "seq", split_axis=0, concat_axis=0, tiled=True)
+def exchange(rows, groups):
+    flat = rows.reshape(len(groups[0]), 1, -1)
+    flat = lax.all_to_all(
+        flat, "seq", split_axis=0, concat_axis=0, tiled=True, axis_index_groups=groups
+    )
     return flat.reshape(rows.shape)
 
 
 def body(inputs, gate_values, filters, skip_weight, grad_out):
     quarter = (lax.axis_index("seq") >> 5).astype(jnp.int32).reshape(1)
     every_filter = lax.all_gather(filters, "chan", axis=0)
-    leaving = source(inputs, gate_values, grad_out, every_filter)
-    results = middle(exchange(leaving), quarter)
-    returned = exchange(results)
+    mixed = grad_out.astype(F32) * gate_values.astype(F32)
+    signals = jnp.concatenate([inputs.astype(F32), mixed], axis=0)
+    leaving = source(signals, every_filter)
+    everyone = [list(range(BLOCKS))]
+    planes = [[MEMBERS * y + w for w in range(MEMBERS)] for y in range(QUARTERS)]
+    columns = [[MEMBERS * y + w for y in range(QUARTERS)] for w in range(MEMBERS)]
+    segment = exchange(leaving, planes)
+    copies = jnp.concatenate([segment] * QUARTERS, axis=0)
+    results = middle(exchange(copies, columns), quarter)
+    returned = exchange(results, everyone)
     shares = lax.all_to_all(sums(returned), "chan", split_axis=0, concat_axis=0, tiled=True)
     grad_input, grad_gate = final(
         returned, inputs, gate_values, grad_out, skip_weight[:, None]

time: 103 us -> 92.4 us (0.90)
  blocking collectives: 37.2 us -> 63.4 us
  waiting for transfers between devices: 28 us -> 7.67 us
  starting transfers between devices: 23.9 us -> 11.3 us
  Pallas kernels: 10.7 us -> 6.62 us
  other arithmetic: 0 us -> 1.51 us
  local copies, waits for them, and re-layouts: 1.94 us -> 0.73 us
    all_to_all x1 -> x2, blocking collectives: 24.7 us -> 51.6 us  [exchange(): lax.all_to_all(flat, 'seq', split_axis=0, concat_axis=0, tiled=True, axis...]
    all_to_all x1, waiting for transfers between devices: 28 us -> 6.23 us  [exchange(): lax.all_to_all(flat, 'seq', split_axis=0, concat_axis=0, tiled=True, axis...]
    all_to_all x1, starting transfers between devices: 17.2 us -> 4.18 us  [exchange(): lax.all_to_all(flat, 'seq', split_axis=0, concat_axis=0, tiled=True, axis...]
    pallas_call x1, Pallas kernels: 1.54 us -> 0.01 us  [source(): pl.pallas_call(source_kernel, out_shape=jax.ShapeDtypeStruct((6 * MEMBERS...]
    all_to_all x1, waiting for transfers between devices: 0.01 us -> 1.44 us  [body(): lax.all_to_all(sums(returned), 'chan', split_axis=0, concat_axis=0, tiled...]
  transfers between devices with their start and end apart: 2 -> 2, of which waited for: 1 -> 2; matrix products, arithmetic and copies ran while one was open for 1% -> 0% of each run, Pallas kernels for 2% -> 1%
where the time goes in v4:
time: 92.4 us; the launch traced here: 91.9 us
  blocking collectives  63.4 us (69%)
  starting transfers between devices  11.3 us (12%)
  waiting for transfers between devices  7.67 us (8%)
  Pallas kernels  6.62 us (7%)
  other arithmetic  1.51 us (2%)
    all_to_all x2, blocking collectives, exchange(): lax.all_to_all(flat, 'seq', split_axis=0, concat_axis=0, tiled=True, axis...  51.6 us
    all_gather x1, blocking collectives, body(): every_filter = lax.all_gather(filters, 'chan', axis=0)  11.8 us
    all_to_all x1, starting transfers between devices, body(): lax.all_to_all(sums(returned), 'chan', split_axis=0, concat_axis=0, tiled...  7.13 us
    all_to_all x1, waiting for transfers between devices, exchange(): lax.all_to_all(flat, 'seq', split_axis=0, concat_axis=0, tiled=True, axis...  6.23 us
    pallas_call x1, Pallas kernels, middle(): pl.pallas_call(middle_kernel, out_shape=jax.ShapeDtypeStruct((2 * BLOCKS,...  4.19 us
    all_to_all x1, starting transfers between devices, exchange(): lax.all_to_all(flat, 'seq', split_axis=0, concat_axis=0, tiled=True, axis...  4.18 us
  transfers between devices with their start and end apart: 2, of which 2 were waited for; matrix products, arithmetic and copies ran while one was open for 0% of the time, Pallas kernels for 1%

profile of v4, /device:TPU:1, one launch (start us, length us, event | category | flops | bytes accessed | tf_op | source)
XLA Modules:
  0.0 91.9 jit_solution(2124539940850826375)
XLA Ops:
  0.6 0.0 copy-start.3
  0.6 0.0 copy-start.1
  0.7 0.0 copy-start.2
  0.7 0.7 convert_element_type.9
  1.4 0.0 copy-done.3
  1.4 11.8 %all-gather.1.filter_ref = f32[4,2,256]{2,1,0:T(2,128)S(1)} all-gather(f32[1,2,256]{2,1,0:T(2,128)S(1)} %bitcast.15), channel_id=2, replica_groups=mesh['seq'=128,'chan'=4] {'chan'}, dimensions={0}, use_global_device_ids=true | all-gather | bytes 10240 | tf_op jit(solution)/shard_map/all_gather | solution.py:267
  13.2 0.0 copy-done.1
  13.2 0.0 copy-done.2
  13.3 27.9 %all_to_all.20 = f32[32,1,768]{2,1,0:T(1,128)S(1)} all-to-all(f32[32,1,768]{2,1,0:T(1,128)S(1)} %bitcast.13), channel_id=1, replica_groups={{0,4,8,12,16,20,24,28,32,36,40,44,48,52,56,60,64,68,72,76,80,84,88,92,9..., dimensions={0} | all-to-all | bytes 196608 | tf_op jit(solution)/shard_map/all_to_all | solution.py:259
  41.2 0.8 pad_maximum_fusion
  41.9 4.2 %all-to-all-start.1 = ((f32[4,1,24576]{2,1,0:T(1,128)}), f32[4,1,24576]{2,1,0:T(1,128)S(1)}, u32[]{:S(2)}, u32[]{:S(2)}) async-start(f32[4,1,24576]{2,1,0:T(1,128)} %bitcast.4), calls=%async_computation.1 | async-start | bytes 786432 | tf_op jit(solution)/shard_map/all_to_all | solution.py:259
  46.1 6.2 %all-to-all-done.1 = f32[4,1,24576]{2,1,0:T(1,128)S(1)} async-done(((f32[4,1,24576]{2,1,0:T(1,128)}), f32[4,1,24576]{2,1,0:T(1,128)S(1)}, u32[]{:S(2)}, u32[]{:S(2)}) %all-to-all-start.1) | async-done | bytes 393248 | tf_op jit(solution)/shard_map/all_to_all | solution.py:259
  52.4 4.2 %shard_map.77 = f32[256,128]{1,0:T(8,128)S(1)} custom-call(s32[1]{0:T(128)} %bitcast.r_ref, f32[768,128]{1,0:T(8,128)S(1)} %bitcast.9), custom_call_target="tpu_custom_call" | custom-call | tf_op jit(solution)/shard_map/pallas_call | solution.py:138
  56.6 23.7 %all_to_all.21 = f32[128,1,256]{2,1,0:T(1,128)S(1)} all-to-all(f32[128,1,256]{2,1,0:T(1,128)S(1)} %bitcast.12), channel_id=1, replica_groups={{0,4,8,12,16,20,24,28,32,36,40,44,48,52,56,60,64,68,72,76,80,84,88,92,9..., dimensions={0} | all-to-all | bytes 262144 | tf_op jit(solution)/shard_map/all_to_all | solution.py:259
  80.2 0.6 shard_map.79
  80.8 0.0 copy-start.4
  80.8 7.1 %all-to-all-start.3 = ((f32[4,8,128]{2,1,0:T(8,128)}), f32[4,8,128]{2,1,0:T(8,128)S(1)}, u32[]{:S(2)}, u32[]{:S(2)}) async-start(f32[4,8,128]{2,1,0:T(8,128)} %shard_map.79), calls=%async_computation.3 | async-start | bytes 32768 | tf_op jit(solution)/shard_map/all_to_all | solution.py:278
  88.0 0.0 copy-start
  88.0 0.0 copy-done.4
  88.0 0.1 copy.11.skip_ref
  88.1 0.6 copy-done
  88.7 1.0 %shard_map.78 = (bf16[32,256]{1,0:T(8,128)(2,1)}, bf16[32,256]{1,0:T(8,128)(2,1)}) custom-call(f32[256,128]{1,0:T(8,128)S(1)} %bitcast.11, bf16[32,256]{1,0:T(8,128)(2,1)S(1)} %copy-done, bf16[32,256]{1,0:T(8,128)(2,1)S(1)} %copy-done.1, bf16[32,256]{1,0:T(8,128)(2,1)S(1)} %copy-done.2, f32[32,1]{1,0:T(8,128)S(1)} %copy.11.skip_ref), custom_call_target="tpu_custom_call" | custom-call | tf_op jit(solution)/shard_map/pallas_call | solution.py:248
  89.7 1.4 %all-to-all-done.3.b_ref = f32[4,8,128]{2,1,0:T(8,128)S(1)} async-done(((f32[4,8,128]{2,1,0:T(8,128)}), f32[4,8,128]{2,1,0:T(8,128)S(1)}, u32[]{:S(2)}, u32[]{:S(2)}) %all-to-all-start.3) | async-done | bytes 16416 | tf_op jit(solution)/shard_map/all_to_all | solution.py:278
  91.1 0.8 shard_map.80
  (3 shorter events, 0.0 us)
Async XLA Ops:
  0.6 0.8 copy-start.3
  0.6 12.6 %copy-start.1 = (bf16[32,256]{1,0:T(8,128)(2,1)S(1)}, bf16[32,256]{1,0:T(8,128)(2,1)}, u32[]{:S(2)}) copy-start(bf16[32,256]{1,0:T(8,128)(2,1)} %gate_ref.1) | copy-start | bytes 49156
  0.7 12.6 %copy-start.2 = (bf16[32,256]{1,0:T(8,128)(2,1)S(1)}, bf16[32,256]{1,0:T(8,128)(2,1)}, u32[]{:S(2)}) copy-start(bf16[32,256]{1,0:T(8,128)(2,1)} %up_ref.1) | copy-start | bytes 49156
  41.9 10.4 %all-to-all-start.1 = ((f32[4,1,24576]{2,1,0:T(1,128)}), f32[4,1,24576]{2,1,0:T(1,128)S(1)}, u32[]{:S(2)}, u32[]{:S(2)}) async-start(f32[4,1,24576]{2,1,0:T(1,128)} %bitcast.4), calls=%async_computation.1 | async-start | bytes 786432 | tf_op jit(solution)/shard_map/all_to_all | solution.py:259
  80.8 7.1 %copy-start.4 = (f32[32]{0:T(128)S(1)}, f32[32]{0:T(128)}, u32[]{:S(2)}) copy-start(f32[32]{0:T(128)} %param.8) | copy-start | bytes 388
  80.8 10.3 %all-to-all-start.3 = ((f32[4,8,128]{2,1,0:T(8,128)}), f32[4,8,128]{2,1,0:T(8,128)S(1)}, u32[]{:S(2)}, u32[]{:S(2)}) async-start(f32[4,8,128]{2,1,0:T(8,128)} %shard_map.79), calls=%async_computation.3 | async-start | bytes 32768 | tf_op jit(solution)/shard_map/all_to_all | solution.py:278
  88.0 0.7 copy-start

commit v5 on v4

--- a/solution.py
+++ b/solution.py
@@ -50,11 +50,33 @@
 def middle_kernel(r_ref, a_ref, out_ref, taps, windows, acc):
     r = r_ref[0]
 
-    def signal(first):
-        halves = [a_ref[pl.ds(first + half, BLOCKS, stride=6), :] for half in range(2)]
-        return jnp.concatenate(halves, axis=1)
-
-    x, g, h = signal(0), signal(2), signal(4)
+    lane = lax.broadcasted_iota(jnp.int32, (MEMBERS, 128), 1) < 64
+
+    def join(even, odd):
+        first = jnp.where(lane, even, pltpu.roll(odd, 64, 1))
+        return first, jnp.where(lane, pltpu.roll(even, 64, 1), odd)
+
+    rows_x, rows_g, rows_h = [], [], []
+    for y in range(QUARTERS):
+        tiles_x, tiles_g, tiles_h = [], [], []
+        for part in (0, 2):
+            even, odd = 4 * y + part, 4 * y + part + 1
+            tile_x, tile_g = join(a_ref[even, :MEMBERS], a_ref[odd, :MEMBERS])
+            tile_h = jnp.where(
+                lane[:16], a_ref[even, MEMBERS:], pltpu.roll(a_ref[odd, MEMBERS:], 64, 1)
+            )
+            tile_i = jnp.where(
+                lane[:16], pltpu.roll(a_ref[even, MEMBERS:], 64, 1), a_ref[odd, MEMBERS:]
+            )
+            tiles_x.append(tile_x)
+            tiles_g.append(tile_g)
+            tiles_h.append(jnp.concatenate([tile_h, tile_i], axis=0))
+        rows_x.append(jnp.concatenate(tiles_x, axis=1))
+        rows_g.append(jnp.concatenate(tiles_g, axis=1))
+        rows_h.append(jnp.concatenate(tiles_h, axis=1))
+    x = jnp.concatenate(rows_x, axis=0)
+    g = jnp.concatenate(rows_g, axis=0)
+    h = jnp.concatenate(rows_h, axis=0)
     h_down = rows_down(h)
 
     def keep(slot):
@@ -80,9 +102,9 @@
     x_down = rows_down(x)
     taps_of(0, jnp.concatenate([h_down[:, 128:], h], axis=1), lambda n: n, 1)
     taps_of(2, jnp.concatenate([x_down[:, 128:], x], axis=1), lambda n: n)
-    lane = lax.broadcasted_iota(jnp.int32, (BLOCK, BLOCK), 1)
-    row = lax.broadcasted_iota(jnp.int32, (BLOCK, BLOCK), 0)
-    mirror = (lane + row == BLOCK - 1).astype(BF16)
+    ahead = lax.broadcasted_iota(jnp.int32, (BLOCK, BLOCK), 1)
+    below = lax.broadcasted_iota(jnp.int32, (BLOCK, BLOCK), 0)
+    mirror = (ahead + below == BLOCK - 1).astype(BF16)
     flipped = jnp.dot(x.astype(BF16), mirror, preferred_element_type=F32)
     flipped_down = rows_down(flipped)
     wide = jnp.concatenate([flipped, flipped_down[:, :128]], axis=1)
@@ -157,24 +179,53 @@
 MEMBERS = 32
 
 
-def source_kernel(signal_ref, filter_ref, out_ref):
-    filters = jnp.concatenate([filter_ref[i] for i in range(4)] * 4, axis=0)
-    line = 0
-    for value in (signal_ref[:MEMBERS], signal_ref[MEMBERS:], filters):
-        for half in range(2):
-            part = value[:, 128 * half : 128 * half + 128]
-            out_ref[pl.ds(line, MEMBERS, stride=6), :] = part
-            line += 1
-
-
-def source(signals, filters):
+def source_kernel(signal_ref, out_ref):
+    lane = lax.broadcasted_iota(jnp.int32, (MEMBERS, 128), 1) < 64
+    x, g = signal_ref[:MEMBERS], signal_ref[MEMBERS : 2 * MEMBERS]
+    h = jnp.concatenate([signal_ref[2 * MEMBERS :]] * 4, axis=0)
+    for part in range(4):
+        at = 128 * (part // 2)
+        px, pg, ph = x[:, at : at + 128], g[:, at : at + 128], h[:, at : at + 128]
+        if part % 2 == 0:
+            pg = pltpu.roll(pg, 64, 1)
+        else:
+            px, ph = pltpu.roll(px, 64, 1), pltpu.roll(ph, 64, 1)
+        out_ref[pl.ds(2 * part, MEMBERS, stride=8), :] = jnp.where(lane, px, pg)
+        out_ref[pl.ds(2 * part + 1, MEMBERS, stride=8), :] = ph
+
+
+def source(signals):
     return pl.pallas_call(
         source_kernel,
-        out_shape=jax.ShapeDtypeStruct((6 * MEMBERS, 128), F32),
-        in_specs=[VMEM] * 2,
+        out_shape=jax.ShapeDtypeStruct((8 * MEMBERS, 128), F32),
+        in_specs=[VMEM],
         out_specs=VMEM,
         compiler_params=SMALL,
-    )(signals, filters)
+    )(signals)
+
+
+def spread_kernel(owner_ref, in_ref, out_ref):
+    owner = owner_ref[0]
+    taps = in_ref[pl.ds(1, MEMBERS, stride=8), :]
+    for slot in range(1, 4):
+        taps = jnp.where(owner == slot, in_ref[pl.ds(2 * slot + 1, MEMBERS, stride=8), :], taps)
+    lane = lax.broadcasted_iota(jnp.int32, (16, 128), 1) < 64
+    packed = jnp.where(lane, taps[:16], pltpu.roll(taps[16:], 64, 1))
+    for slot in range(4):
+        tokens = in_ref[pl.ds(2 * slot, MEMBERS, stride=8), :]
+        for y in range(QUARTERS):
+            out_ref[4 * y + slot, :MEMBERS] = tokens
+            out_ref[4 * y + slot, MEMBERS:] = packed
+
+
+def spread(owner, segment):
+    return pl.pallas_call(
+        spread_kernel,
+        out_shape=jax.ShapeDtypeStruct((16, 48, 128), F32),
+        in_specs=[pl.BlockSpec(memory_space=pltpu.SMEM), VMEM],
+        out_specs=VMEM,
+        compiler_params=SMALL,
+    )(owner, segment)
 
 
 def exact_dot(value, pick):
@@ -257,24 +308,37 @@
 def exchange(rows, groups):
     flat = rows.reshape(len(groups[0]), 1, -1)
     flat = lax.all_to_all(
-        flat, "seq", split_axis=0, concat_axis=0, tiled=True, axis_index_groups=groups
+        flat, ("seq", "chan"), split_axis=0, concat_axis=0, tiled=True, axis_index_groups=groups
     )
     return flat.reshape(rows.shape)
 
 
 def body(inputs, gate_values, filters, skip_weight, grad_out):
-    quarter = (lax.axis_index("seq") >> 5).astype(jnp.int32).reshape(1)
-    every_filter = lax.all_gather(filters, "chan", axis=0)
+    def device(y, w, slot):
+        return 4 * (MEMBERS * y + w) + slot
+
+    planes = [
+        [device(y, w, slot) for w in range(MEMBERS) for slot in range(4)]
+        for y in range(QUARTERS)
+    ]
+    columns = [
+        [device(y, w, slot) for y in range(QUARTERS) for slot in range(4)]
+        for w in range(MEMBERS)
+    ]
+    slots = [
+        [device(y, w, slot) for y in range(QUARTERS) for w in range(MEMBERS)]
+        for slot in range(4)
+    ]
+    place = lax.axis_index("seq").astype(jnp.int32)
+    quarter = (place >> 5).reshape(1)
+    owner = ((place >> 1) & 3).reshape(1)
     mixed = grad_out.astype(F32) * gate_values.astype(F32)
-    signals = jnp.concatenate([inputs.astype(F32), mixed], axis=0)
-    leaving = source(signals, every_filter)
-    everyone = [list(range(BLOCKS))]
-    planes = [[MEMBERS * y + w for w in range(MEMBERS)] for y in range(QUARTERS)]
-    columns = [[MEMBERS * y + w for y in range(QUARTERS)] for w in range(MEMBERS)]
-    segment = exchange(leaving, planes)
-    copies = jnp.concatenate([segment] * QUARTERS, axis=0)
-    results = middle(exchange(copies, columns), quarter)
-    returned = exchange(results, everyone)
+    pairs = jnp.concatenate([filters] * 4, axis=0)
+    signals = jnp.concatenate([inputs.astype(F32), mixed, pairs], axis=0)
+    signals, quarter, owner = lax.optimization_barrier((signals, quarter, owner))
+    segment = exchange(source(signals), planes)
+    results = middle(exchange(spread(owner, segment), columns), quarter)
+    returned = exchange(results, slots)
     shares = lax.all_to_all(sums(returned), "chan", split_axis=0, concat_axis=0, tiled=True)
     grad_input, grad_gate = final(
         returned, inputs, gate_values, grad_out, skip_weight[:, None]

time: 92.4 us -> 93.2 us (level)
  blocking collectives: 63.4 us -> 76.2 us
  waiting for transfers between devices: 7.67 us -> 1.44 us
  starting transfers between devices: 11.3 us -> 5.91 us
    all_to_all x2 -> x3, blocking collectives: 51.6 us -> 76.2 us  [exchange(): lax.all_to_all(flat, ('seq', 'chan'), split_axis=0, concat_axis=0, tiled=...]
    all_gather x1 -> x0, blocking collectives: 11.8 us -> none  [body(): every_filter = lax.all_gather(filters, 'chan', axis=0)]
    all_to_all x1 -> x0, waiting for transfers between devices: 6.23 us -> none  [exchange(): lax.all_to_all(flat, 'seq', split_axis=0, concat_axis=0, tiled=True, axis...]
    all_to_all x1 -> x0, starting transfers between devices: 4.18 us -> none  [exchange(): lax.all_to_all(flat, 'seq', split_axis=0, concat_axis=0, tiled=True, axis...]
    all_to_all x1, starting transfers between devices: 7.13 us -> 5.91 us  [body(): lax.all_to_all(sums(returned), 'chan', split_axis=0, concat_axis=0, tiled...]
  transfers between devices with their start and end apart: 2 -> 1, of which waited for: 2 -> 1; matrix products, arithmetic and copies ran while one was open for 0% -> 0% of each run, Pallas kernels for 1% -> 1%
where the time goes in v5:
time: 93.2 us; the launch traced here: 92.7 us
  blocking collectives  76.2 us (82%)
  Pallas kernels  6.99 us (8%)
  starting transfers between devices  5.91 us (6%)
  waiting for transfers between devices  1.44 us (2%)
    all_to_all x3, blocking collectives, exchange(): lax.all_to_all(flat, ('seq', 'chan'), split_axis=0, concat_axis=0, tiled=...  76.2 us
    all_to_all x1, starting transfers between devices, body(): lax.all_to_all(sums(returned), 'chan', split_axis=0, concat_axis=0, tiled...  5.91 us
    pallas_call x1, Pallas kernels, middle(): pl.pallas_call(middle_kernel, out_shape=jax.ShapeDtypeStruct((2 * BLOCKS,...  4.4 us
  transfers between devices with their start and end apart: 1, of which 1 were waited for; matrix products, arithmetic and copies ran while one was open for 0% of the time, Pallas kernels for 1%

profile of v5, /device:TPU:1, one launch (start us, length us, event | category | flops | bytes accessed | tf_op | source)
XLA Modules:
  0.0 92.7 jit_solution(8297670549331039708)
XLA Ops:
  0.6 0.0 copy-start.2
  0.6 0.0 copy-start.3
  0.7 0.8 convert_multiply_fusion
  1.4 0.0 copy-done.2
  1.4 0.0 copy-done.3
  1.5 0.1 shard_map.76
  1.6 36.7 %all_to_all.20 = f32[128,1,256]{2,1,0:T(1,128)S(1)} all-to-all(f32[128,1,256]{2,1,0:T(1,128)S(1)} %bitcast.15), channel_id=1, replica_groups={{0,1,2,3,4,5,6,7,8,9,10,11,12,13,14,15,16,17,18,19,20,21,22,23,24,25,26..., dimensions={0} | all-to-all | bytes 262144 | tf_op jit(solution)/shard_map/all_to_all | solution.py:310
  38.2 0.1 shard_map.77
  38.3 14.6 %all_to_all.21 = f32[16,1,6144]{2,1,0:T(1,128)S(1)} all-to-all(f32[16,1,6144]{2,1,0:T(1,128)S(1)} %bitcast.9), channel_id=1, replica_groups={{0,1,2,3,128,129,130,131,256,257,258,259,384,385,386,387},{4,5,6,7,132,..., dimensions={0} | all-to-all | bytes 786432 | tf_op jit(solution)/shard_map/all_to_all | solution.py:310
  52.9 4.4 %shard_map.78 = f32[256,128]{1,0:T(8,128)S(1)} custom-call(s32[1]{0:T(128)} %bitcast.r_ref, f32[16,48,128]{2,1,0:T(8,128)S(1)} %bitcast.10), custom_call_target="tpu_custom_call" | custom-call | tf_op jit(solution)/shard_map/pallas_call | solution.py:160
  57.3 25.0 %all_to_all.22 = f32[128,1,256]{2,1,0:T(1,128)S(1)} all-to-all(f32[128,1,256]{2,1,0:T(1,128)S(1)} %bitcast.14), channel_id=1, replica_groups={{0,4,8,12,16,20,24,28,32,36,40,44,48,52,56,60,64,68,72,76,80,84,88,92,9..., dimensions={0} | all-to-all | bytes 262144 | tf_op jit(solution)/shard_map/all_to_all | solution.py:310
  82.3 0.6 shard_map.80
  82.9 0.0 copy-start.4
  82.9 0.0 copy-start.1
  82.9 5.9 %all-to-all-start.3 = ((f32[4,8,128]{2,1,0:T(8,128)}), f32[4,8,128]{2,1,0:T(8,128)S(1)}, u32[]{:S(2)}, u32[]{:S(2)}) async-start(f32[4,8,128]{2,1,0:T(8,128)} %shard_map.80), calls=%async_computation.3 | async-start | bytes 32768 | tf_op jit(solution)/shard_map/all_to_all | solution.py:342
  88.8 0.0 copy-start
  88.8 0.0 copy-done.4
  88.8 0.1 copy.12.skip_ref
  88.9 0.0 copy-done.1
  88.9 0.6 copy-done
  89.5 1.0 %shard_map.79 = (bf16[32,256]{1,0:T(8,128)(2,1)}, bf16[32,256]{1,0:T(8,128)(2,1)}) custom-call(f32[256,128]{1,0:T(8,128)S(1)} %bitcast.12, bf16[32,256]{1,0:T(8,128)(2,1)S(1)} %copy-done.2, bf16[32,256]{1,0:T(8,128)(2,1)S(1)} %copy-done, bf16[32,256]{1,0:T(8,128)(2,1)S(1)} %copy-done.1, f32[32,1]{1,0:T(8,128)S(1)} %copy.12.skip_ref), custom_call_target="tpu_custom_call" | custom-call | tf_op jit(solution)/shard_map/pallas_call | solution.py:299
  90.5 1.4 %all-to-all-done.3.b_ref = f32[4,8,128]{2,1,0:T(8,128)S(1)} async-done(((f32[4,8,128]{2,1,0:T(8,128)}), f32[4,8,128]{2,1,0:T(8,128)S(1)}, u32[]{:S(2)}, u32[]{:S(2)}) %all-to-all-start.3) | async-done | bytes 16416 | tf_op jit(solution)/shard_map/all_to_all | solution.py:342
  91.9 0.8 shard_map.81
  (1 shorter events, 0.0 us)
Async XLA Ops:
  0.6 0.8 copy-start.2
  0.6 0.8 copy-start.3
  82.9 5.9 %copy-start.4 = (f32[32]{0:T(128)S(1)}, f32[32]{0:T(128)}, u32[]{:S(2)}) copy-start(f32[32]{0:T(128)} %param.8) | copy-start | bytes 388
  82.9 6.0 %copy-start.1 = (bf16[32,256]{1,0:T(8,128)(2,1)S(1)}, bf16[32,256]{1,0:T(8,128)(2,1)}, u32[]{:S(2)}) copy-start(bf16[32,256]{1,0:T(8,128)(2,1)} %up_ref.1) | copy-start | bytes 49156
  82.9 9.0 %all-to-all-start.3 = ((f32[4,8,128]{2,1,0:T(8,128)}), f32[4,8,128]{2,1,0:T(8,128)S(1)}, u32[]{:S(2)}, u32[]{:S(2)}) async-start(f32[4,8,128]{2,1,0:T(8,128)} %shard_map.80), calls=%async_computation.3 | async-start | bytes 32768 | tf_op jit(solution)/shard_map/all_to_all | solution.py:342
  88.8 0.7 copy-start

commit v6 on v4

--- a/solution.py
+++ b/solution.py
@@ -77,33 +77,18 @@
             if low_slot is not None:
                 taps[low_slot, :, n] = low.reshape(STEPS, FINE, BLOCK)
 
-    x_down = rows_down(x)
-    taps_of(0, jnp.concatenate([h_down[:, 128:], h], axis=1), lambda n: n, 1)
-    taps_of(2, jnp.concatenate([x_down[:, 128:], x], axis=1), lambda n: n)
-    lane = lax.broadcasted_iota(jnp.int32, (BLOCK, BLOCK), 1)
-    row = lax.broadcasted_iota(jnp.int32, (BLOCK, BLOCK), 0)
-    mirror = (lane + row == BLOCK - 1).astype(BF16)
-    flipped = jnp.dot(x.astype(BF16), mirror, preferred_element_type=F32)
-    flipped_down = rows_down(flipped)
-    wide = jnp.concatenate([flipped, flipped_down[:, :128]], axis=1)
-    taps_of(3, pltpu.roll(wide, 128, 1), lambda n: n - (FINE - 1))
-
-    for step in range(STEPS):
-        shift = FINE * step
-        size = BLOCKS - shift
-
-        def rhs(slot):
-            return taps[slot, step].reshape(BLOCK, BLOCK)
-
-        def lhs(slot, start):
-            return windows[slot, :, start : start + size].reshape(PARTS * size, BLOCK)
-
-        g_high, g_low = lhs(0, shift), lhs(1, shift)
-        h_high, h_low = lhs(2, 0), lhs(3, 0)
-        cross = nt_dot(g_high, rhs(2)) + nt_dot(g_low, rhs(2))
-        pulled = nt_dot(g_high, rhs(0)) + nt_dot(g_low, rhs(0)) + nt_dot(g_high, rhs(1))
-        conv = nt_dot(h_high, rhs(3)) + nt_dot(h_low, rhs(3))
-        for slot, start, value in ((0, shift, conv), (1, 0, pulled), (2, 0, cross)):
+    def products(slot, left, right, down, extra=None):
+        for step in range(STEPS):
+            shift = FINE * step
+            size = BLOCKS - shift
+            begin, start = (0, shift) if down else (shift, 0)
+            both = windows[left : left + 2, :, begin : begin + size]
+            both = both.reshape(2 * PARTS * size, BLOCK)
+            value = nt_dot(both, taps[right, step].reshape(BLOCK, BLOCK))
+            value = value[: PARTS * size] + value[PARTS * size :]
+            if extra is not None:
+                high = both[: PARTS * size]
+                value = value + nt_dot(high, taps[extra, step].reshape(BLOCK, BLOCK))
             value = value.reshape(PARTS, size, BLOCK)
             if step == 0:
                 acc[slot] = value
@@ -114,13 +99,13 @@
     line = lax.broadcasted_iota(jnp.int32, (BLOCKS, BLOCK), 0)
     source = lax.broadcasted_iota(jnp.int32, (BLOCK, 128), 0)
     target = lax.broadcasted_iota(jnp.int32, (BLOCK, 128), 1)
-    totals = [jnp.zeros((BLOCKS, 128), F32), jnp.zeros((BLOCKS, 128), F32)]
-    for slot, page, offset in ((0, 0, 0), (1, 0, 64), (2, 1, 0)):
-        total = totals[page]
+
+    def collected(slot, down, offset):
+        total = jnp.zeros((BLOCKS, 128), F32)
         for i in range(PARTS):
             value = acc[slot, i]
             for bit in (1, 2, 4, 8):
-                if slot == 0:
+                if down:
                     moved = jnp.where(line < bit, 0.0, pltpu.roll(value, bit, 0))
                 else:
                     moved = jnp.where(line >= BLOCKS - bit, 0.0, pltpu.roll(value, BLOCKS - bit, 0))
@@ -129,9 +114,27 @@
             high, low = split(value)
             total = total + jnp.dot(high, pick, preferred_element_type=F32)
             total = total + jnp.dot(low, pick, preferred_element_type=F32)
-        totals[page] = total
-    out_ref[pl.ds(0, BLOCKS, stride=2), :] = totals[0]
-    out_ref[pl.ds(1, BLOCKS, stride=2), :] = totals[1]
+        return total
+
+    x_down = rows_down(x)
+    lane = lax.broadcasted_iota(jnp.int32, (BLOCK, BLOCK), 1)
+    row = lax.broadcasted_iota(jnp.int32, (BLOCK, BLOCK), 0)
+    mirror = (lane + row == BLOCK - 1).astype(BF16)
+    flipped = jnp.dot(x.astype(BF16), mirror, preferred_element_type=F32)
+    flipped_down = rows_down(flipped)
+    wide = jnp.concatenate([flipped, flipped_down[:, :128]], axis=1)
+    taps_of(3, pltpu.roll(wide, 128, 1), lambda n: n - (FINE - 1))
+
+    taps_of(0, jnp.concatenate([h_down[:, 128:], h], axis=1), lambda n: n, 1)
+    taps_of(2, jnp.concatenate([x_down[:, 128:], x], axis=1), lambda n: n)
+    products(0, 2, 3, True)
+    products(1, 0, 0, False, extra=1)
+    products(2, 0, 2, False)
+    conv = collected(0, True, 0)
+    pulled = collected(1, False, 64)
+    cross = collected(2, False, 0)
+    out_ref[pl.ds(0, BLOCKS, stride=2), :] = conv + pulled
+    out_ref[pl.ds(1, BLOCKS, stride=2), :] = cross
 
 
 def middle(arrived, r):
@@ -163,14 +166,16 @@
     for value in (signal_ref[:MEMBERS], signal_ref[MEMBERS:], filters):
         for half in range(2):
             part = value[:, 128 * half : 128 * half + 128]
-            out_ref[pl.ds(line, MEMBERS, stride=6), :] = part
+            for quarter in range(QUARTERS):
+                start = 6 * MEMBERS * quarter + line
+                out_ref[pl.ds(start, MEMBERS, stride=6), :] = part
             line += 1
 
 
 def source(signals, filters):
     return pl.pallas_call(
         source_kernel,
-        out_shape=jax.ShapeDtypeStruct((6 * MEMBERS, 128), F32),
+        out_shape=jax.ShapeDtypeStruct((6 * BLOCKS, 128), F32),
         in_specs=[VMEM] * 2,
         out_specs=VMEM,
         compiler_params=SMALL,
@@ -254,27 +259,20 @@
     )(returned, x, gate, up, skip)
 
 
-def exchange(rows, groups):
-    flat = rows.reshape(len(groups[0]), 1, -1)
-    flat = lax.all_to_all(
-        flat, "seq", split_axis=0, concat_axis=0, tiled=True, axis_index_groups=groups
-    )
+def exchange(rows):
+    flat = rows.reshape(BLOCKS, 1, -1)
+    flat = lax.all_to_all(flat, "seq", split_axis=0, concat_axis=0, tiled=True)
     return flat.reshape(rows.shape)
 
 
 def body(inputs, gate_values, filters, skip_weight, grad_out):
     quarter = (lax.axis_index("seq") >> 5).astype(jnp.int32).reshape(1)
-    every_filter = lax.all_gather(filters, "chan", axis=0)
     mixed = grad_out.astype(F32) * gate_values.astype(F32)
     signals = jnp.concatenate([inputs.astype(F32), mixed], axis=0)
-    leaving = source(signals, every_filter)
-    everyone = [list(range(BLOCKS))]
-    planes = [[MEMBERS * y + w for w in range(MEMBERS)] for y in range(QUARTERS)]
-    columns = [[MEMBERS * y + w for y in range(QUARTERS)] for w in range(MEMBERS)]
-    segment = exchange(leaving, planes)
-    copies = jnp.concatenate([segment] * QUARTERS, axis=0)
-    results = middle(exchange(copies, columns), quarter)
-    returned = exchange(results, everyone)
+    every_filter = lax.all_gather(filters, "chan", axis=0)
+    signals, quarter = lax.optimization_barrier((signals, quarter))
+    results = middle(exchange(source(signals, every_filter)), quarter)
+    returned = exchange(results)
     shares = lax.all_to_all(sums(returned), "chan", split_axis=0, concat_axis=0, tiled=True)
     grad_input, grad_gate = final(
         returned, inputs, gate_values, grad_out, skip_weight[:, None]

time: 92.4 us -> 98.5 us (1.066)
  blocking collectives: 63.4 us -> 81 us
  waiting for transfers between devices: 7.67 us -> 1.44 us
  starting transfers between devices: 11.3 us -> 6.76 us
    all_to_all x2, blocking collectives: 51.6 us -> 69.2 us  [exchange(): flat = lax.all_to_all(flat, 'seq', split_axis=0, concat_axis=0, tiled=True)]
    all_to_all x1 -> x0, waiting for transfers between devices: 6.23 us -> none  [exchange(): lax.all_to_all(flat, 'seq', split_axis=0, concat_axis=0, tiled=True, axis...]
    all_to_all x1 -> x0, starting transfers between devices: 4.18 us -> none  [exchange(): lax.all_to_all(flat, 'seq', split_axis=0, concat_axis=0, tiled=True, axis...]
  transfers between devices with their start and end apart: 2 -> 1, of which waited for: 2 -> 1; matrix products, arithmetic and copies ran while one was open for 0% -> 0% of each run, Pallas kernels for 1% -> 1%
where the time goes in v6:
time: 98.5 us; the launch traced here: 98 us
  blocking collectives  81 us (82%)
  starting transfers between devices  6.76 us (7%)
  Pallas kernels  5.88 us (6%)
  waiting for transfers between devices  1.44 us (1%)
  local copies, waits for them, and re-layouts  1.4 us (1%)
    all_to_all x2, blocking collectives, exchange(): flat = lax.all_to_all(flat, 'seq', split_axis=0, concat_axis=0, tiled=True)  69.2 us
    all_gather x1, blocking collectives, body(): every_filter = lax.all_gather(filters, 'chan', axis=0)  11.8 us
    all_to_all x1, starting transfers between devices, body(): lax.all_to_all(sums(returned), 'chan', split_axis=0, concat_axis=0, tiled...  6.76 us
    pallas_call x1, Pallas kernels, middle(): pl.pallas_call(middle_kernel, out_shape=jax.ShapeDtypeStruct((2 * BLOCKS,...  3.44 us
  transfers between devices with their start and end apart: 1, of which 1 were waited for; matrix products, arithmetic and copies ran while one was open for 0% of the time, Pallas kernels for 1%

profile of v6, /device:TPU:1, one launch (start us, length us, event | category | flops | bytes accessed | tf_op | source)
XLA Modules:
  0.0 98.0 jit_solution(4106639112972261214)
XLA Ops:
  0.6 0.0 copy-start.1
  0.6 0.0 copy-start.2
  0.7 0.7 convert_element_type.9
  1.4 0.0 copy-done.1
  1.4 0.0 copy-done.2
  1.4 0.0 copy-start.3
  1.4 0.7 copy-done.3
  2.1 11.8 %all-gather.1.filter_ref = f32[4,2,256]{2,1,0:T(2,128)S(1)} all-gather(f32[1,2,256]{2,1,0:T(2,128)S(1)} %bitcast.12), channel_id=2, replica_groups=mesh['seq'=128,'chan'=4] {'chan'}, dimensions={0}, use_global_device_ids=true | all-gather | bytes 10240 | tf_op jit(solution)/shard_map/all_gather | solution.py:272
  14.0 44.6 %all_to_all.15 = f32[128,1,768]{2,1,0:T(1,128)S(1)} all-to-all(f32[128,1,768]{2,1,0:T(1,128)S(1)} %bitcast.7), channel_id=1, replica_groups=mesh['seq'=128,'chan'=4] {'seq'}, dimensions={0} | all-to-all | bytes 786432 | tf_op jit(solution)/shard_map/all_to_all | solution.py:264
  58.6 3.4 %shard_map.77 = f32[256,128]{1,0:T(8,128)S(1)} custom-call(s32[1]{0:T(128)} %bitcast.r_ref, f32[768,128]{1,0:T(8,128)S(1)} %bitcast.8), custom_call_target="tpu_custom_call" | custom-call | tf_op jit(solution)/shard_map/pallas_call | solution.py:141
  62.0 24.6 %all_to_all.16 = f32[128,1,256]{2,1,0:T(1,128)S(1)} all-to-all(f32[128,1,256]{2,1,0:T(1,128)S(1)} %bitcast.11), channel_id=1, replica_groups=mesh['seq'=128,'chan'=4] {'seq'}, dimensions={0} | all-to-all | bytes 262144 | tf_op jit(solution)/shard_map/all_to_all | solution.py:264
  86.6 0.6 shard_map.79
  87.2 0.0 copy-start.4
  87.2 6.8 %all-to-all-start.2 = ((f32[4,8,128]{2,1,0:T(8,128)}), f32[4,8,128]{2,1,0:T(8,128)S(1)}, u32[]{:S(2)}, u32[]{:S(2)}) async-start(f32[4,8,128]{2,1,0:T(8,128)} %shard_map.79), calls=%async_computation.2 | async-start | bytes 32768 | tf_op jit(solution)/shard_map/all_to_all | solution.py:276
  94.0 0.0 copy-start
  94.0 0.0 copy-done.4
  94.0 0.1 copy.11.skip_ref
  94.1 0.6 copy-done
  94.7 1.0 shard_map.78
  95.7 1.4 %all-to-all-done.2.b_ref = f32[4,8,128]{2,1,0:T(8,128)S(1)} async-done(((f32[4,8,128]{2,1,0:T(8,128)}), f32[4,8,128]{2,1,0:T(8,128)S(1)}, u32[]{:S(2)}, u32[]{:S(2)}) %all-to-all-start.2) | async-done | bytes 16416 | tf_op jit(solution)/shard_map/all_to_all | solution.py:276
  97.1 0.8 shard_map.80
  (3 shorter events, 0.0 us)
Async XLA Ops:
  0.6 0.8 copy-start.1
  0.6 0.7 copy-start.2
  1.4 0.7 copy-start.3
  87.2 6.8 %copy-start.4 = (f32[32]{0:T(128)S(1)}, f32[32]{0:T(128)}, u32[]{:S(2)}) copy-start(f32[32]{0:T(128)} %param.8) | copy-start | bytes 388
  87.2 9.9 %all-to-all-start.2 = ((f32[4,8,128]{2,1,0:T(8,128)}), f32[4,8,128]{2,1,0:T(8,128)S(1)}, u32[]{:S(2)}, u32[]{:S(2)}) async-start(f32[4,8,128]{2,1,0:T(8,128)} %shard_map.79), calls=%async_computation.2 | async-start | bytes 32768 | tf_op jit(solution)/shard_map/all_to_all | solution.py:276
  94.0 0.7 copy-start

commit v7 on v6

--- a/solution.py
+++ b/solution.py
@@ -51,7 +51,7 @@
     r = r_ref[0]
 
     def signal(first):
-        halves = [a_ref[pl.ds(first + half, BLOCKS, stride=6), :] for half in range(2)]
+        halves = [a_ref[:, first + half].reshape(BLOCKS, 128) for half in range(2)]
         return jnp.concatenate(halves, axis=1)
 
     x, g, h = signal(0), signal(2), signal(4)
@@ -157,29 +157,54 @@
 
 VMEM = pl.BlockSpec(memory_space=pltpu.VMEM)
 SMALL = pltpu.CompilerParams(vmem_limit_bytes=4 * 1024 * 1024)
-MEMBERS = 32
-
-
-def source_kernel(signal_ref, filter_ref, out_ref):
-    filters = jnp.concatenate([filter_ref[i] for i in range(4)] * 4, axis=0)
+RING = 16
+PLANES = 8
+
+
+def source_kernel(signal_ref, filter_ref, skip_ref, out_ref, aside_ref):
+    filters = jnp.concatenate([filter_ref[i] for i in range(4)] * 2, axis=0)
     line = 0
-    for value in (signal_ref[:MEMBERS], signal_ref[MEMBERS:], filters):
+    for value in [signal_ref[RING * i : RING * i + RING] for i in range(4)] + [filters]:
         for half in range(2):
             part = value[:, 128 * half : 128 * half + 128]
-            for quarter in range(QUARTERS):
-                start = 6 * MEMBERS * quarter + line
-                out_ref[pl.ds(start, MEMBERS, stride=6), :] = part
+            out_ref[pl.ds(line, RING, stride=10), :] = part
             line += 1
-
-
-def source(signals, filters):
+    across = lax.broadcasted_iota(jnp.int32, (32, 32), 1)
+    down = lax.broadcasted_iota(jnp.int32, (32, 32), 0)
+    skip = jnp.where(across == down, skip_ref[...], 0.0).sum(axis=1, keepdims=True)
+    aside_ref[...] = jnp.broadcast_to(skip, aside_ref.shape)
+
+
+def source(signals, filters, skip):
     return pl.pallas_call(
         source_kernel,
-        out_shape=jax.ShapeDtypeStruct((6 * BLOCKS, 128), F32),
-        in_specs=[VMEM] * 2,
+        out_shape=(
+            jax.ShapeDtypeStruct((10 * RING, 128), F32),
+            jax.ShapeDtypeStruct((32, BLOCK), F32),
+        ),
+        in_specs=[VMEM] * 3,
+        out_specs=[VMEM] * 2,
+        compiler_params=SMALL,
+    )(signals, filters, skip)
+
+
+def spread_kernel(in_ref, out_ref):
+    lines = [in_ref[pl.ds(line, RING, stride=10), :] for line in range(10)]
+    for plane in range(PLANES):
+        member = plane % 2
+        chosen = (2 * member, 2 * member + 1, 4 + 2 * member, 5 + 2 * member, 8, 9)
+        for place, line in enumerate(chosen):
+            out_ref[plane, place] = lines[line]
+
+
+def spread(ring):
+    return pl.pallas_call(
+        spread_kernel,
+        out_shape=jax.ShapeDtypeStruct((PLANES, 6, RING, 128), F32),
+        in_specs=[VMEM],
         out_specs=VMEM,
         compiler_params=SMALL,
-    )(signals, filters)
+    )(ring)
 
 
 def exact_dot(value, pick):
@@ -200,84 +225,88 @@
 
 
 def sums_kernel(b_ref, out_ref):
+    lane = lax.broadcasted_iota(jnp.int32, (8, 128), 1) < 64
+    totals = []
     for quarter in range(QUARTERS):
         rows = b_ref[pl.ds(64 * quarter + 1, 32, stride=2), :]
-        total = rows.reshape(4, 8, 128).sum(axis=0)
-        for owner in range(4):
-            out_ref[owner, 2 * quarter : 2 * quarter + 2] = total[2 * owner : 2 * owner + 2]
+        totals.append(rows.reshape(4, 8, 128).sum(axis=0))
+    for k in range(2):
+        out_ref[k] = jnp.where(lane, totals[2 * k], pltpu.roll(totals[2 * k + 1], 64, 1))
 
 
 def sums(returned):
     return pl.pallas_call(
         sums_kernel,
-        out_shape=jax.ShapeDtypeStruct((4, 8, 128), F32),
+        out_shape=jax.ShapeDtypeStruct((2, 8, 128), F32),
         in_specs=[VMEM],
         out_specs=VMEM,
         compiler_params=SMALL,
     )(returned)
 
 
-def taps_kernel(b_ref, gf_ref):
-    taps = jnp.zeros((2, BLOCK), F32)
-    cross = (b_ref[0] + b_ref[1]) + (b_ref[2] + b_ref[3])
-    for quarter in range(QUARTERS):
-        taps = taps + exact_dot(cross[2 * quarter : 2 * quarter + 2], quarter_pick(quarter, BLOCK))
-    gf_ref[...] = taps * (1.0 / math.sqrt(BLOCKS * BLOCK))
-
-
-def final_taps(parts):
-    return pl.pallas_call(
-        taps_kernel,
-        out_shape=jax.ShapeDtypeStruct((2, BLOCK), F32),
-        in_specs=[VMEM],
-        out_specs=VMEM,
-        compiler_params=SMALL,
-    )(parts)
-
-
-def final_kernel(b_ref, x_ref, gate_ref, up_ref, skip_ref, gi_ref, gg_ref):
+def final_kernel(slot_ref, b_ref, signal_ref, up_ref, skip_ref, shares_ref, gi_ref, gg_ref, gf_ref):
     both = jnp.zeros((32, 2 * BLOCK), F32)
     for quarter in range(QUARTERS):
         rows = b_ref[pl.ds(64 * quarter, 32, stride=2), :]
         both = both + exact_dot(rows, quarter_pick(quarter, 2 * BLOCK))
-    x = x_ref[...].astype(F32)
-    up = up_ref[...].astype(F32)
-    mixed = up * gate_ref[...].astype(F32)
-    skip = skip_ref[...]
+    x, mixed = signal_ref[:32], signal_ref[32:]
+    up, skip = up_ref[...].astype(F32), skip_ref[...]
     gg_ref[...] = (up * (both[:, :BLOCK] + skip * x)).astype(BF16)
     gi_ref[...] = (both[:, BLOCK:] + skip * mixed).astype(BF16)
 
-
-def final(returned, x, gate, up, skip):
+    source = lax.broadcasted_iota(jnp.int32, (128, BLOCK), 0)
+    target = lax.broadcasted_iota(jnp.int32, (128, BLOCK), 1)
+    taps = jnp.zeros((8, BLOCK), F32)
+    for k in range(2):
+        total = (shares_ref[0, k] + shares_ref[1, k]) + (shares_ref[2, k] + shares_ref[3, k])
+        token = source % 64
+        place = (token // FINE) * (BLOCK // PARTS) + FINE * (2 * k + source // 64) + token % FINE
+        taps = taps + exact_dot(total, (place == target).astype(BF16))
+    slot = slot_ref[0]
+    own = taps[:2]
+    for other in range(1, 4):
+        own = jnp.where(slot == other, taps[2 * other : 2 * other + 2], own)
+    gf_ref[...] = own * (1.0 / math.sqrt(BLOCKS * BLOCK))
+
+
+def final(slot, returned, signals, upstream, skip, shares):
     piece = jax.ShapeDtypeStruct((32, BLOCK), BF16)
     return pl.pallas_call(
         final_kernel,
-        out_shape=(piece, piece),
-        in_specs=[VMEM] * 5,
-        out_specs=[VMEM] * 2,
+        out_shape=(piece, piece, jax.ShapeDtypeStruct((2, BLOCK), F32)),
+        in_specs=[pl.BlockSpec(memory_space=pltpu.SMEM)] + [VMEM] * 5,
+        out_specs=[VMEM] * 3,
         compiler_params=SMALL,
-    )(returned, x, gate, up, skip)
-
-
-def exchange(rows):
-    flat = rows.reshape(BLOCKS, 1, -1)
-    flat = lax.all_to_all(flat, "seq", split_axis=0, concat_axis=0, tiled=True)
+    )(slot, returned, signals, upstream, skip, shares)
+
+
+def exchange(rows, groups=None):
+    members = BLOCKS if groups is None else len(groups[0])
+    flat = lax.all_to_all(
+        rows.reshape(members, 1, -1),
+        "seq",
+        split_axis=0,
+        concat_axis=0,
+        tiled=True,
+        axis_index_groups=groups,
+    )
     return flat.reshape(rows.shape)
 
 
 def body(inputs, gate_values, filters, skip_weight, grad_out):
-    quarter = (lax.axis_index("seq") >> 5).astype(jnp.int32).reshape(1)
+    rings = [[RING * plane + z for z in range(RING)] for plane in range(PLANES)]
+    planes = [[RING * plane + z for plane in range(PLANES)] for z in range(RING)]
     mixed = grad_out.astype(F32) * gate_values.astype(F32)
     signals = jnp.concatenate([inputs.astype(F32), mixed], axis=0)
     every_filter = lax.all_gather(filters, "chan", axis=0)
-    signals, quarter = lax.optimization_barrier((signals, quarter))
-    results = middle(exchange(source(signals, every_filter)), quarter)
-    returned = exchange(results)
-    shares = lax.all_to_all(sums(returned), "chan", split_axis=0, concat_axis=0, tiled=True)
-    grad_input, grad_gate = final(
-        returned, inputs, gate_values, grad_out, skip_weight[:, None]
-    )
-    return (grad_input, grad_gate, final_taps(shares))
+    leaving, skip = source(signals, every_filter, skip_weight[None, :])
+    quarter = (lax.axis_index("seq") >> 5).astype(jnp.int32).reshape(1)
+    slot = lax.axis_index("chan").astype(jnp.int32).reshape(1)
+    leaving, quarter, slot = lax.optimization_barrier((leaving, quarter, slot))
+    arrived = exchange(spread(exchange(leaving, rings)), planes)
+    returned = exchange(middle(arrived, quarter))
+    shares = lax.all_gather(sums(returned), "chan", axis=0)
+    return final(slot, returned, signals, grad_out, skip, shares)
 
 
 def solution(mesh):

time: 98.5 us -> 88.6 us (0.90)
  starting transfers between devices: 6.76 us -> 0 us
  waiting for transfers between devices: 1.44 us -> 0 us
  Pallas kernels: 5.88 us -> 4.67 us
    all_gather x0 -> x1, blocking collectives: none -> 8.6 us  [body(): shares = lax.all_gather(sums(returned), 'chan', axis=0)]
    all_to_all x2 -> x3, blocking collectives: 69.2 us -> 60.9 us  [exchange(): lax.all_to_all(rows.reshape(members, 1, -1), 'seq', split_axis=0, concat_...]
    all_to_all x1 -> x0, starting transfers between devices: 6.76 us -> none  [body(): lax.all_to_all(sums(returned), 'chan', split_axis=0, concat_axis=0, tiled...]
    all_to_all x1 -> x0, waiting for transfers between devices: 1.44 us -> none  [body(): lax.all_to_all(sums(returned), 'chan', split_axis=0, concat_axis=0, tiled...]
    pallas_call x4, Pallas kernels: 2.44 us -> 1.22 us  [the longest x1 1.03 us: final(): pl.pallas_call(final_kernel, out_shape=(piece, piece, jax.ShapeDtypeStruc...]
  transfers between devices with their start and end apart: 1 -> 0, of which waited for: 1 -> 0; matrix products, arithmetic and copies ran while one was open for 0% -> 0% of each run, Pallas kernels for 1% -> 0%
where the time goes in v7:
time: 88.6 us; the launch traced here: 88.2 us
  blocking collectives  81.4 us (92%)
  Pallas kernels  4.67 us (5%)
  local copies, waits for them, and re-layouts  1.37 us (2%)
    all_to_all x3, blocking collectives, exchange(): lax.all_to_all(rows.reshape(members, 1, -1), 'seq', split_axis=0, concat_...  60.9 us
    all_gather x1, blocking collectives, body(): every_filter = lax.all_gather(filters, 'chan', axis=0)  12 us
    all_gather x1, blocking collectives, body(): shares = lax.all_gather(sums(returned), 'chan', axis=0)  8.6 us
    pallas_call x1, Pallas kernels, middle(): pl.pallas_call(middle_kernel, out_shape=jax.ShapeDtypeStruct((2 * BLOCKS,...  3.45 us

profile of v7, /device:TPU:1, one launch (start us, length us, event | category | flops | bytes accessed | tf_op | source)
XLA Modules:
  0.0 88.2 jit_solution(8434965451046009961)
XLA Ops:
  0.6 0.0 copy-start.2
  0.6 12.0 %all-gather.2.filter_ref = f32[4,2,256]{2,1,0:T(2,128)S(1)} all-gather(f32[1,2,256]{2,1,0:T(2,128)} %bitcast.20), channel_id=2, replica_groups=mesh['seq'=128,'chan'=4] {'chan'}, dimensions={0}, use_global_device_ids=true | all-gather | bytes 10240 | tf_op jit(solution)/shard_map/all_gather | solution.py:301
  12.6 0.0 copy-done.2
  12.6 0.0 copy-start
  12.6 0.0 copy-start.3
  12.6 0.7 copy-done
  13.3 0.0 copy-done.3
  13.4 0.0 copy-start.1
  13.4 0.6 copy-done.1
  14.0 0.1 shard_map.76
  14.1 21.3 %all_to_all.15 = f32[16,1,1280]{2,1,0:T(1,128)S(1)} all-to-all(f32[16,1,1280]{2,1,0:T(1,128)S(1)} %bitcast.18), channel_id=1, replica_groups={{0,4,8,12,16,20,24,28,32,36,40,44,48,52,56,60},{64,68,72,76,80,84,88,92..., dimensions={0} | all-to-all | bytes 163840 | tf_op jit(solution)/shard_map/all_to_all | solution.py:285
  35.4 15.0 %all_to_all.16 = f32[8,1,12288]{2,1,0:T(1,128)S(1)} all-to-all(f32[8,1,12288]{2,1,0:T(1,128)S(1)} %bitcast.12), channel_id=1, replica_groups={{0,64,128,192,256,320,384,448},{4,68,132,196,260,324,388,452},{8,72,136..., dimensions={0} | all-to-all | bytes 786432 | tf_op jit(solution)/shard_map/all_to_all | solution.py:285
  50.4 3.5 %shard_map.78 = f32[256,128]{1,0:T(8,128)S(1)} custom-call(s32[1]{0:T(128)} %bitcast.2.r_ref, f32[8,6,16,128]{3,2,1,0:T(8,128)S(1)} %bitcast.11), custom_call_target="tpu_custom_call" | custom-call | tf_op jit(solution)/shard_map/pallas_call | solution.py:141
  53.9 24.6 %all_to_all.17 = f32[128,1,256]{2,1,0:T(1,128)S(1)} all-to-all(f32[128,1,256]{2,1,0:T(1,128)S(1)} %bitcast.15), channel_id=1, replica_groups=mesh['seq'=128,'chan'=4] {'seq'}, dimensions={0} | all-to-all | bytes 262144 | tf_op jit(solution)/shard_map/all_to_all | solution.py:285
  78.5 0.1 shard_map.79
  78.5 8.6 %all-gather.1 = f32[8,8,128]{2,1,0:T(8,128)S(1)} all-gather(f32[2,8,128]{2,1,0:T(8,128)S(1)} %shard_map.79), channel_id=3, replica_groups=mesh['seq'=128,'chan'=4] {'chan'}, dimensions={0}, use_global_device_ids=true | all-gather | bytes 40960 | tf_op jit(solution)/shard_map/all_gather | solution.py:308
  87.1 1.0 %shard_map.80 = (bf16[32,256]{1,0:T(8,128)(2,1)}, bf16[32,256]{1,0:T(8,128)(2,1)}, f32[2,256]{1,0:T(2,128)}) custom-call(s32[1]{0:T(128)} %bitcast.3.slot_ref, f32[256,128]{1,0:T(8,128)S(1)} %bitcast.14, f32[64,256]{1,0:T(8,128)S(1)} %pad_maximum_fusion.signal_ref, bf16[32,256]{1,0:T(8,128)(2,1)S(1)} %copy-done, f32[32,256]{1,0:T(8,128)S(1)} %get-tuple-element.12.skip_ref, ...), custom_call_target="tpu_custom_call" | custom-call | tf_op jit(solution)/shard_map/pallas_call | solution.py:274
  (4 shorter events, 0.0 us)
Async XLA Ops:
  0.6 12.0 %copy-start.2 = (bf16[32,256]{1,0:T(8,128)(2,1)S(1)}, bf16[32,256]{1,0:T(8,128)(2,1)}, u32[]{:S(2)}) copy-start(bf16[32,256]{1,0:T(8,128)(2,1)} %param.5) | copy-start | bytes 49156
  12.6 0.7 copy-start
  12.6 0.7 copy-start.3
  13.4 0.7 copy-start.1

commit v8 on v7

v8 whole, which is shorter than its diff:
```python
import functools
import math

import jax
import jax.numpy as jnp
from jax import lax
from jax.experimental import pallas as pl
from jax.experimental.pallas import tpu as pltpu
from jax.sharding import PartitionSpec as P

BLOCK = 256
BLOCKS = 128
FINE = 16
PARTS = BLOCK // FINE
RING = 16
PLANES = 8
F32 = jnp.float32
BF16 = jnp.bfloat16


def split(value):
    high = value.astype(BF16)
    return high, (value - high.astype(F32)).astype(BF16)


def rows_down(value):
    row = lax.broadcasted_iota(jnp.int32, value.shape, 0)
    return jnp.where(row == 0, 0.0, pltpu.roll(value, 1, 0))


def rows_up(value):
    row = lax.broadcasted_iota(jnp.int32, value.shape, 0)
    return jnp.where(row == BLOCKS - 1, 0.0, pltpu.roll(value, BLOCKS - 1, 0))


def nt_dot(left, right):
    return lax.dot_general(
        left, right, (((1,), (1,)), ((), ())), preferred_element_type=F32
    )


def middle_kernel(plane_ref, a_ref, out_ref, h_wide, x_wide, f_wide, g_ext, x_ext, taps, ahead, behind, acc):
    plane = plane_ref[0]

    def signal(first):
        halves = [a_ref[:, first + half].reshape(BLOCKS, 128) for half in range(2)]
        return jnp.concatenate(halves, axis=1)

    def runs(value):
        return value.reshape(PLANES, RING, value.shape[1])

    h = signal(8)
    h_down = rows_down(h)
    across = lax.broadcasted_iota(jnp.int32, (BLOCK, BLOCK), 1)
    down = lax.broadcasted_iota(jnp.int32, (BLOCK, BLOCK), 0)
    mirror = (across + down == BLOCK - 1).astype(BF16)
    for place, piece in enumerate(split(h)):
        flipped = jnp.dot(piece, mirror, preferred_element_type=F32)
        wide = jnp.concatenate([rows_down(flipped)[:, :128], flipped], axis=1)
        f_wide[place] = runs(wide.astype(BF16))
    for place, piece in enumerate(split(jnp.concatenate([h_down[:, 128:], h], axis=1))):
        h_wide[place] = runs(piece)
    for member in range(2):
        x = signal(2 * member)
        g = signal(4 + 2 * member)
        x_down = rows_down(x)
        x_wide[member] = runs(jnp.concatenate([x_down[:, 128:], x], axis=1).astype(BF16))
        x_ext[member] = runs(jnp.concatenate([x_down, x], axis=1).astype(BF16))
        for place, piece in enumerate(split(jnp.concatenate([g, rows_up(g)], axis=1))):
            g_ext[member, place] = runs(piece)

    def turn(value, shift):
        size = value.shape[1]
        return pltpu.roll(value, shift % size, 1) if shift % size else value

    def taps_of(slot, wide, step, least):
        for n in range(FINE):
            taps[slot, step, n] = turn(wide, least + n)[:, 128:]

    def ahead_taps(step):
        for place in range(2):
            taps_of(place, h_wide[place, step], step, 0)
            taps_of(2 + place, x_wide[place, step], step, 0)

    def behind_taps(step):
        for place in range(2):
            taps_of(4 + place, f_wide[place, step], step, 1 - FINE)

    size = PARTS * RING

    def rhs(slot, step):
        return taps[slot, step].reshape(BLOCK, BLOCK)

    def pulled_and_cross(lhs, step):
        high = nt_dot(lhs, rhs(0, step))
        pulled, cross = [], None
        for member in range(2):
            at = 2 * size * member
            low = nt_dot(lhs[at : at + size], rhs(1, step))
            pulled.append(high[at : at + size] + high[at + size : at + 2 * size] + low)
            both = nt_dot(lhs[at : at + 2 * size], rhs(2 + member, step))
            both = both[:size] + both[size:]
            cross = both if cross is None else cross + both
        return pulled[0], pulled[1], cross

    def convolved(lhs, step):
        both = nt_dot(lhs, rhs(4, step)) + nt_dot(lhs, rhs(5, step))
        return both[:size], both[size:]

    def ahead_step(step):
        for member in range(2):
            for place in range(2):
                wide = g_ext[member, place, plane + step]
                for i in range(PARTS):
                    ahead[member, place, i] = turn(wide, -FINE * i)[:, :BLOCK]
        lhs = ahead[...].reshape(4 * size, BLOCK)
        if step:
            for k, value in enumerate(pulled_and_cross(lhs, step - 1)):
                acc[1, 2 + k] += value
        for k, value in enumerate(pulled_and_cross(lhs, step)):
            if step:
                acc[0, 2 + k] += value
            else:
                acc[0, 2 + k] = value
                acc[1, 2 + k] = jnp.zeros((size, BLOCK), F32)
        if step + 1 < PLANES:
            ahead_taps(step + 1)

    def behind_step(step):
        for member in range(2):
            wide = x_ext[member, plane - step]
            for i in range(PARTS):
                behind[member, i] = turn(wide, -FINE * (i + 1))[:, :BLOCK]
        lhs = behind[...].reshape(2 * size, BLOCK)
        if step:
            for k, value in enumerate(convolved(lhs, step - 1)):
                acc[1, k] += value
        for k, value in enumerate(convolved(lhs, step)):
            if step:
                acc[0, k] += value
            else:
                acc[0, k] = value
                acc[1, k] = jnp.zeros((size, BLOCK), F32)
        if step + 1 < PLANES:
            behind_taps(step + 1)

    ahead_taps(0)
    behind_taps(0)
    ahead_step(0)
    behind_step(0)
    for step in range(1, PLANES):
        pl.when(step < PLANES - plane)(functools.partial(ahead_step, step))
    for step in range(1, PLANES):
        pl.when(step <= plane)(functools.partial(behind_step, step))

    lanes = lax.broadcasted_iota(jnp.int32, (RING, BLOCK), 1) % FINE
    lines = lax.broadcasted_iota(jnp.int32, (RING, BLOCK), 0)
    source = lax.broadcasted_iota(jnp.int32, (BLOCK, BLOCK), 0) // FINE
    target = lax.broadcasted_iota(jnp.int32, (BLOCK, BLOCK), 1)
    total = jnp.zeros((5 * RING, BLOCK), F32)
    for i in range(PARTS):
        pieces = []
        for k in range(5):
            near = acc[0, k, RING * i : RING * i + RING]
            far = acc[1, k, RING * i : RING * i + RING]
            value = jnp.where(lines + lanes < RING if k < 2 else lines >= lanes, near, far)
            for bit in (1, 2, 4, 8):
                moved = pltpu.roll(value, bit if k < 2 else RING - bit, 0)
                value = jnp.where((lanes & bit) != 0, moved, value)
            pieces.append(value)
        pick = (source + FINE * i == target).astype(BF16)
        high, low = split(jnp.concatenate(pieces, axis=0))
        total = total + jnp.dot(high, pick, preferred_element_type=F32)
        total = total + jnp.dot(low, pick, preferred_element_type=F32)
    for k in range(5):
        for half in range(2):
            part = total[RING * k : RING * k + RING, 128 * half : 128 * half + 128]
            out_ref[pl.ds(2 * k + half, RING, stride=10), :] = part


def middle(arrived, plane):
    return pl.pallas_call(
        middle_kernel,
        out_shape=jax.ShapeDtypeStruct((10 * RING, 128), F32),
        in_specs=[
            pl.BlockSpec(memory_space=pltpu.SMEM),
            pl.BlockSpec(memory_space=pltpu.VMEM),
        ],
        out_specs=pl.BlockSpec(memory_space=pltpu.VMEM),
        scratch_shapes=[
            pltpu.VMEM((2, PLANES, RING, 384), BF16),
            pltpu.VMEM((2, PLANES, RING, 384), BF16),
            pltpu.VMEM((2, PLANES, RING, 384), BF16),
            pltpu.VMEM((2, 2, PLANES, RING, 2 * BLOCK), BF16),
            pltpu.VMEM((2, PLANES, RING, 2 * BLOCK), BF16),
            pltpu.VMEM((6, PLANES, FINE, FINE, BLOCK), BF16),
            pltpu.VMEM((2, 2, PARTS, RING, BLOCK), BF16),
            pltpu.VMEM((2, PARTS, RING, BLOCK), BF16),
            pltpu.VMEM((2, 5, PARTS * RING, BLOCK), F32),
        ],
        compiler_params=pltpu.CompilerParams(vmem_limit_bytes=32 * 1024 * 1024),
    )(plane, arrived)


VMEM = pl.BlockSpec(memory_space=pltpu.VMEM)
SMALL = pltpu.CompilerParams(vmem_limit_bytes=4 * 1024 * 1024)


def source_kernel(signal_ref, filter_ref, skip_ref, out_ref, aside_ref):
    filters = jnp.concatenate([filter_ref[i] for i in range(4)] * 2, axis=0)
    line = 0
    for value in [signal_ref[RING * i : RING * i + RING] for i in range(4)] + [filters]:
        for half in range(2):
            part = value[:, 128 * half : 128 * half + 128]
            out_ref[pl.ds(line, RING, stride=10), :] = part
            line += 1
    across = lax.broadcasted_iota(jnp.int32, (32, 32), 1)
    down = lax.broadcasted_iota(jnp.int32, (32, 32), 0)
    skip = jnp.where(across == down, skip_ref[...], 0.0).sum(axis=1, keepdims=True)
    aside_ref[...] = jnp.broadcast_to(skip, aside_ref.shape)


def source(signals, filters, skip):
    return pl.pallas_call(
        source_kernel,
        out_shape=(
            jax.ShapeDtypeStruct((10 * RING, 128), F32),
            jax.ShapeDtypeStruct((32, BLOCK), F32),
        ),
        in_specs=[VMEM] * 3,
        out_specs=[VMEM] * 2,
        compiler_params=SMALL,
    )(signals, filters, skip)


def spread_kernel(in_ref, out_ref):
    for line in range(10):
        rows = in_ref[pl.ds(line, RING, stride=10), :]
        for plane in range(PLANES):
            out_ref[plane, line] = rows


def spread(ring):
    return pl.pallas_call(
        spread_kernel,
        out_shape=jax.ShapeDtypeStruct((PLANES, 10, RING, 128), F32),
        in_specs=[VMEM],
        out_specs=VMEM,
        compiler_params=SMALL,
    )(ring)


def sums_kernel(b_ref, out_ref):
    for half in range(2):
        rows = b_ref[pl.ds(8 + half, RING, stride=10), :]
        out_ref[:, 128 * half : 128 * half + 128] = rows[:8] + rows[8:]


def sums(returned):
    return pl.pallas_call(
        sums_kernel,
        out_shape=jax.ShapeDtypeStruct((8, BLOCK), F32),
        in_specs=[VMEM],
        out_specs=VMEM,
        compiler_params=SMALL,
    )(returned)


def final_kernel(slot_ref, b_ref, signal_ref, up_ref, skip_ref, shares_ref, gi_ref, gg_ref, gf_ref):
    def channels(first):
        halves = [
            jnp.concatenate(
                [b_ref[pl.ds(first + 2 * member + half, RING, stride=10), :] for member in range(2)],
                axis=0,
            )
            for half in range(2)
        ]
        return jnp.concatenate(halves, axis=1)

    x, mixed = signal_ref[:32], signal_ref[32:]
    up, skip = up_ref[...].astype(F32), skip_ref[...]
    gg_ref[...] = (up * (channels(0) + skip * x)).astype(BF16)
    gi_ref[...] = (channels(4) + skip * mixed).astype(BF16)
    taps = (shares_ref[0] + shares_ref[1]) + (shares_ref[2] + shares_ref[3])
    slot = slot_ref[0]
    own = taps[:2]
    for other in range(1, 4):
        own = jnp.where(slot == other, taps[2 * other : 2 * other + 2], own)
    gf_ref[...] = own * (1.0 / math.sqrt(BLOCKS * BLOCK))


def final(slot, returned, signals, upstream, skip, shares):
    piece = jax.ShapeDtypeStruct((32, BLOCK), BF16)
    return pl.pallas_call(
        final_kernel,
        out_shape=(piece, piece, jax.ShapeDtypeStruct((2, BLOCK), F32)),
        in_specs=[pl.BlockSpec(memory_space=pltpu.SMEM)] + [VMEM] * 5,
        out_specs=[VMEM] * 3,
        compiler_params=SMALL,
    )(slot, returned, signals, upstream, skip, shares)


def exchange(rows, groups=None):
    members = BLOCKS if groups is None else len(groups[0])
    flat = lax.all_to_all(
        rows.reshape(members, 1, -1),
        "seq",
        split_axis=0,
        concat_axis=0,
        tiled=True,
        axis_index_groups=groups,
    )
    return flat.reshape(rows.shape)


def body(inputs, gate_values, filters, skip_weight, grad_out):
    rings = [[RING * plane + z for z in range(RING)] for plane in range(PLANES)]
    planes = [[RING * plane + z for plane in range(PLANES)] for z in range(RING)]
    mixed = grad_out.astype(F32) * gate_values.astype(F32)
    signals = jnp.concatenate([inputs.astype(F32), mixed], axis=0)
    every_filter = lax.all_gather(filters, "chan", axis=0)
    leaving, skip = source(signals, every_filter, skip_weight[None, :])
    plane = (lax.axis_index("seq") >> 4).astype(jnp.int32).reshape(1)
    slot = lax.axis_index("chan").astype(jnp.int32).reshape(1)
    leaving, plane, slot = lax.optimization_barrier((leaving, plane, slot))
    arrived = exchange(spread(exchange(leaving, rings)), planes)
    returned = exchange(middle(arrived, plane), rings)
    shares = lax.all_gather(sums(returned), "chan", axis=0)
    return final(slot, returned, signals, grad_out, skip, shares)


def solution(mesh):
    placed = (P("chan", "seq"), P("chan", "seq"), P("chan", "seq"), P("chan"), P("chan", "seq"))
    return jax.shard_map(
        body,
        mesh=mesh,
        in_specs=placed,
        out_specs=(P("chan", "seq"), P("chan", "seq"), P("chan", "seq")),
        check_vma=False,
    )
```

time: 88.6 us -> 87.7 us (0.990)
  blocking collectives: 81.4 us -> 75.9 us
  Pallas kernels: 4.67 us -> 9.28 us
    all_to_all x3, blocking collectives: 60.9 us -> 55 us  [exchange(): lax.all_to_all(rows.reshape(members, 1, -1), 'seq', split_axis=0, concat_...]
    pallas_call x3, Pallas kernels: 3.55 us -> 8.57 us  [the longest x1 8.52 us: middle(): pl.pallas_call(middle_kernel, out_shape=jax.ShapeDtypeStruct((10 * RING,...]
where the time goes in v8:
time: 87.7 us; the launch traced here: 87.3 us
  blocking collectives  75.9 us (87%)
  Pallas kernels  9.28 us (11%)
  local copies, waits for them, and re-layouts  1.37 us (2%)
    all_to_all x3, blocking collectives, exchange(): lax.all_to_all(rows.reshape(members, 1, -1), 'seq', split_axis=0, concat_...  55 us
    all_gather x1, blocking collectives, body(): every_filter = lax.all_gather(filters, 'chan', axis=0)  12 us
    all_gather x1, blocking collectives, body(): shares = lax.all_gather(sums(returned), 'chan', axis=0)  9 us
    pallas_call x1, Pallas kernels, middle(): pl.pallas_call(middle_kernel, out_shape=jax.ShapeDtypeStruct((10 * RING,...  8.52 us

profile of v8, /device:TPU:1, one launch (start us, length us, event | category | flops | bytes accessed | tf_op | source)
XLA Modules:
  0.0 87.3 jit_solution(10368866451741681606)
XLA Ops:
  0.6 0.0 copy-start.2
  0.6 12.0 %all-gather.2.filter_ref = f32[4,2,256]{2,1,0:T(2,128)S(1)} all-gather(f32[1,2,256]{2,1,0:T(2,128)} %bitcast.20), channel_id=2, replica_groups=mesh['seq'=128,'chan'=4] {'chan'}, dimensions={0}, use_global_device_ids=true | all-gather | bytes 10240 | tf_op jit(solution)/shard_map/all_gather | solution.py:321
  12.6 0.0 copy-done.2
  12.6 0.0 copy-start
  12.6 0.0 copy-start.3
  12.6 0.7 copy-done
  13.3 0.0 copy-done.3
  13.4 0.0 copy-start.1
  13.4 0.6 copy-done.1
  14.0 0.1 shard_map.76
  14.1 21.3 %all_to_all.15 = f32[16,1,1280]{2,1,0:T(1,128)S(1)} all-to-all(f32[16,1,1280]{2,1,0:T(1,128)S(1)} %bitcast.18), channel_id=1, replica_groups={{0,4,8,12,16,20,24,28,32,36,40,44,48,52,56,60},{64,68,72,76,80,84,88,92..., dimensions={0} | all-to-all | bytes 163840 | tf_op jit(solution)/shard_map/all_to_all | solution.py:305
  35.4 16.7 %all_to_all.16 = f32[8,1,20480]{2,1,0:T(1,128)S(1)} all-to-all(f32[8,1,20480]{2,1,0:T(1,128)S(1)} %bitcast.12), channel_id=1, replica_groups={{0,64,128,192,256,320,384,448},{4,68,132,196,260,324,388,452},{8,72,136..., dimensions={0} | all-to-all | bytes 1310720 | tf_op jit(solution)/shard_map/all_to_all | solution.py:305
  52.1 8.5 %shard_map.78 = f32[160,128]{1,0:T(8,128)S(1)} custom-call(s32[1]{0:T(128)} %bitcast.2.plane_ref, f32[8,10,16,128]{3,2,1,0:T(8,128)S(1)} %bitcast.11), custom_call_target="tpu_custom_call" | custom-call | tf_op jit(solution)/shard_map/pallas_call | solution.py:182
  60.6 17.0 %all_to_all.17 = f32[16,1,1280]{2,1,0:T(1,128)S(1)} all-to-all(f32[16,1,1280]{2,1,0:T(1,128)S(1)} %bitcast.15), channel_id=1, replica_groups={{0,4,8,12,16,20,24,28,32,36,40,44,48,52,56,60},{64,68,72,76,80,84,88,92..., dimensions={0} | all-to-all | bytes 163840 | tf_op jit(solution)/shard_map/all_to_all | solution.py:305
  77.7 9.0 %all-gather.1 = f32[32,256]{1,0:T(8,128)S(1)} all-gather(f32[8,256]{1,0:T(8,128)S(1)} %shard_map.79), channel_id=3, replica_groups=mesh['seq'=128,'chan'=4] {'chan'}, dimensions={0}, use_global_device_ids=true | all-gather | bytes 40960 | tf_op jit(solution)/shard_map/all_gather | solution.py:328
  86.7 0.6 shard_map.80
  (5 shorter events, 0.1 us)
Async XLA Ops:
  0.6 12.0 %copy-start.2 = (bf16[32,256]{1,0:T(8,128)(2,1)S(1)}, bf16[32,256]{1,0:T(8,128)(2,1)}, u32[]{:S(2)}) copy-start(bf16[32,256]{1,0:T(8,128)(2,1)} %param.5) | copy-start | bytes 49156
  12.6 0.7 copy-start
  12.6 0.7 copy-start.3
  13.4 0.7 copy-start.1

commit v9 on v8

--- a/solution.py
+++ b/solution.py
@@ -107,51 +107,55 @@
         both = nt_dot(lhs, rhs(4, step)) + nt_dot(lhs, rhs(5, step))
         return both[:size], both[size:]
 
-    def ahead_step(step):
+    def ahead_step(step, first):
         for member in range(2):
             for place in range(2):
                 wide = g_ext[member, place, plane + step]
                 for i in range(PARTS):
                     ahead[member, place, i] = turn(wide, -FINE * i)[:, :BLOCK]
         lhs = ahead[...].reshape(4 * size, BLOCK)
-        if step:
+        if not first:
             for k, value in enumerate(pulled_and_cross(lhs, step - 1)):
                 acc[1, 2 + k] += value
         for k, value in enumerate(pulled_and_cross(lhs, step)):
-            if step:
+            if not first:
                 acc[0, 2 + k] += value
             else:
                 acc[0, 2 + k] = value
                 acc[1, 2 + k] = jnp.zeros((size, BLOCK), F32)
-        if step + 1 < PLANES:
-            ahead_taps(step + 1)
-
-    def behind_step(step):
+        ahead_taps(jnp.minimum(step + 1, PLANES - 1) if not first else 1)
+
+    def behind_step(step, first):
         for member in range(2):
             wide = x_ext[member, plane - step]
             for i in range(PARTS):
                 behind[member, i] = turn(wide, -FINE * (i + 1))[:, :BLOCK]
         lhs = behind[...].reshape(2 * size, BLOCK)
-        if step:
+        if not first:
             for k, value in enumerate(convolved(lhs, step - 1)):
                 acc[1, k] += value
         for k, value in enumerate(convolved(lhs, step)):
-            if step:
+            if not first:
                 acc[0, k] += value
             else:
                 acc[0, k] = value
                 acc[1, k] = jnp.zeros((size, BLOCK), F32)
-        if step + 1 < PLANES:
-            behind_taps(step + 1)
+        behind_taps(jnp.minimum(step + 1, PLANES - 1) if not first else 1)
 
     ahead_taps(0)
     behind_taps(0)
-    ahead_step(0)
-    behind_step(0)
-    for step in range(1, PLANES):
-        pl.when(step < PLANES - plane)(functools.partial(ahead_step, step))
-    for step in range(1, PLANES):
-        pl.when(step <= plane)(functools.partial(behind_step, step))
+    ahead_step(0, True)
+    behind_step(0, True)
+    def ahead_loop(step, carry):
+        ahead_step(step, False)
+        return carry
+
+    def behind_loop(step, carry):
+        behind_step(step, False)
+        return carry
+
+    lax.fori_loop(1, PLANES - plane, ahead_loop, 0)
+    lax.fori_loop(1, plane + 1, behind_loop, 0)
 
     lanes = lax.broadcasted_iota(jnp.int32, (RING, BLOCK), 1) % FINE
     lines = lax.broadcasted_iota(jnp.int32, (RING, BLOCK), 0)
@@ -169,9 +173,9 @@
                 value = jnp.where((lanes & bit) != 0, moved, value)
             pieces.append(value)
         pick = (source + FINE * i == target).astype(BF16)
-        high, low = split(jnp.concatenate(pieces, axis=0))
-        total = total + jnp.dot(high, pick, preferred_element_type=F32)
-        total = total + jnp.dot(low, pick, preferred_element_type=F32)
+        both = jnp.concatenate(split(jnp.concatenate(pieces, axis=0)), axis=0)
+        both = jnp.dot(both, pick, preferred_element_type=F32)
+        total = total + (both[: 5 * RING] + both[5 * RING :])
     for k in range(5):
         for half in range(2):
             part = total[RING * k : RING * k + RING, 128 * half : 128 * half + 128]

time: 87.7 us -> 87.5 us (level)
  no operation moved by 1% of the time
where the time goes in v9:
time: 87.5 us; the launch traced here: 87.1 us
  blocking collectives  75.9 us (87%)
  Pallas kernels  9.08 us (10%)
  local copies, waits for them, and re-layouts  1.37 us (2%)
    all_to_all x3, blocking collectives, exchange(): lax.all_to_all(rows.reshape(members, 1, -1), 'seq', split_axis=0, concat_...  54.9 us
    all_gather x1, blocking collectives, body(): every_filter = lax.all_gather(filters, 'chan', axis=0)  12 us
    all_gather x1, blocking collectives, body(): shares = lax.all_gather(sums(returned), 'chan', axis=0)  9 us
    pallas_call x1, Pallas kernels, middle(): pl.pallas_call(middle_kernel, out_shape=jax.ShapeDtypeStruct((10 * RING,...  8.33 us

profile of v9, /device:TPU:1, one launch (start us, length us, event | category | flops | bytes accessed | tf_op | source)
XLA Modules:
  0.0 87.1 jit_solution(12060295681167852085)
XLA Ops:
  0.6 0.0 copy-start.2
  0.6 12.0 %all-gather.2.filter_ref = f32[4,2,256]{2,1,0:T(2,128)S(1)} all-gather(f32[1,2,256]{2,1,0:T(2,128)} %bitcast.20), channel_id=2, replica_groups=mesh['seq'=128,'chan'=4] {'chan'}, dimensions={0}, use_global_device_ids=true | all-gather | bytes 10240 | tf_op jit(solution)/shard_map/all_gather | solution.py:325
  12.6 0.0 copy-done.2
  12.6 0.0 copy-start
  12.6 0.0 copy-start.3
  12.6 0.7 copy-done
  13.3 0.0 copy-done.3
  13.4 0.0 copy-start.1
  13.4 0.6 copy-done.1
  14.0 0.1 shard_map.76
  14.1 21.3 %all_to_all.15 = f32[16,1,1280]{2,1,0:T(1,128)S(1)} all-to-all(f32[16,1,1280]{2,1,0:T(1,128)S(1)} %bitcast.18), channel_id=1, replica_groups={{0,4,8,12,16,20,24,28,32,36,40,44,48,52,56,60},{64,68,72,76,80,84,88,92..., dimensions={0} | all-to-all | bytes 163840 | tf_op jit(solution)/shard_map/all_to_all | solution.py:309
  35.4 16.7 %all_to_all.16 = f32[8,1,20480]{2,1,0:T(1,128)S(1)} all-to-all(f32[8,1,20480]{2,1,0:T(1,128)S(1)} %bitcast.12), channel_id=1, replica_groups={{0,64,128,192,256,320,384,448},{4,68,132,196,260,324,388,452},{8,72,136..., dimensions={0} | all-to-all | bytes 1310720 | tf_op jit(solution)/shard_map/all_to_all | solution.py:309
  52.1 8.3 %shard_map.78 = f32[160,128]{1,0:T(8,128)S(1)} custom-call(s32[1]{0:T(128)} %bitcast.2.plane_ref, f32[8,10,16,128]{3,2,1,0:T(8,128)S(1)} %bitcast.11), custom_call_target="tpu_custom_call" | custom-call | tf_op jit(solution)/shard_map/pallas_call | solution.py:186
  60.4 17.0 %all_to_all.17 = f32[16,1,1280]{2,1,0:T(1,128)S(1)} all-to-all(f32[16,1,1280]{2,1,0:T(1,128)S(1)} %bitcast.15), channel_id=1, replica_groups={{0,4,8,12,16,20,24,28,32,36,40,44,48,52,56,60},{64,68,72,76,80,84,88,92..., dimensions={0} | all-to-all | bytes 163840 | tf_op jit(solution)/shard_map/all_to_all | solution.py:309
  77.4 9.0 %all-gather.1 = f32[32,256]{1,0:T(8,128)S(1)} all-gather(f32[8,256]{1,0:T(8,128)S(1)} %shard_map.79), channel_id=3, replica_groups=mesh['seq'=128,'chan'=4] {'chan'}, dimensions={0}, use_global_device_ids=true | all-gather | bytes 40960 | tf_op jit(solution)/shard_map/all_gather | solution.py:332
  86.4 0.6 shard_map.80
  (5 shorter events, 0.1 us)
Async XLA Ops:
  0.6 12.0 %copy-start.2 = (bf16[32,256]{1,0:T(8,128)(2,1)S(1)}, bf16[32,256]{1,0:T(8,128)(2,1)}, u32[]{:S(2)}) copy-start(bf16[32,256]{1,0:T(8,128)(2,1)} %param.5) | copy-start | bytes 49156
  12.6 0.7 copy-start
  12.6 0.7 copy-start.3
  13.4 0.7 copy-start.1

commit v10 on v9

--- a/solution.py
+++ b/solution.py
@@ -39,15 +39,20 @@
     )
 
 
-def middle_kernel(plane_ref, a_ref, out_ref, h_wide, x_wide, f_wide, g_ext, x_ext, taps, ahead, behind, acc):
+def middle_kernel(plane_ref, a_ref, out_ref, h_wide, x_wide, f_wide, g_ext, x_ext, taps_a, taps_b, ahead, behind, acc):
     plane = plane_ref[0]
 
     def signal(first):
         halves = [a_ref[:, first + half].reshape(BLOCKS, 128) for half in range(2)]
         return jnp.concatenate(halves, axis=1)
 
-    def runs(value):
-        return value.reshape(PLANES, RING, value.shape[1])
+    def turn(value, shift):
+        size = value.shape[1]
+        return pltpu.roll(value, shift % size, 1) if shift % size else value
+
+    def pairs(value, shift):
+        parts = [part.reshape(PLANES, 2, 8, -1) for part in (value, turn(value, shift))]
+        return jnp.concatenate(parts, axis=2)
 
     h = signal(8)
     h_down = rows_down(h)
@@ -57,116 +62,138 @@
     for place, piece in enumerate(split(h)):
         flipped = jnp.dot(piece, mirror, preferred_element_type=F32)
         wide = jnp.concatenate([rows_down(flipped)[:, :128], flipped], axis=1)
-        f_wide[place] = runs(wide.astype(BF16))
-    for place, piece in enumerate(split(jnp.concatenate([h_down[:, 128:], h], axis=1))):
-        h_wide[place] = runs(piece)
+        f_wide[place] = pairs(wide, 1).astype(BF16)
+    for place, piece in enumerate(split(pairs(jnp.concatenate([h_down[:, 128:], h], axis=1), 1))):
+        h_wide[place] = piece
     for member in range(2):
         x = signal(2 * member)
         g = signal(4 + 2 * member)
         x_down = rows_down(x)
-        x_wide[member] = runs(jnp.concatenate([x_down[:, 128:], x], axis=1).astype(BF16))
-        x_ext[member] = runs(jnp.concatenate([x_down, x], axis=1).astype(BF16))
-        for place, piece in enumerate(split(jnp.concatenate([g, rows_up(g)], axis=1))):
-            g_ext[member, place] = runs(piece)
-
-    def turn(value, shift):
-        size = value.shape[1]
-        return pltpu.roll(value, shift % size, 1) if shift % size else value
-
-    def taps_of(slot, wide, step, least):
-        for n in range(FINE):
-            taps[slot, step, n] = turn(wide, least + n)[:, 128:]
-
-    def ahead_taps(step):
+        x_wide[member] = pairs(jnp.concatenate([x_down[:, 128:], x], axis=1), 1).astype(BF16)
+        x_ext[member] = pairs(jnp.concatenate([x_down, x], axis=1), -FINE).astype(BF16)
+        wide = pairs(jnp.concatenate([g, rows_up(g)], axis=1), -FINE)
+        for place, piece in enumerate(split(wide)):
+            g_ext[member, place] = piece
+
+    size = PARTS * 8
+
+    def taps_of(ref, side, slot, wide_ref, place, step, least):
+        for half in range(2):
+            wide = wide_ref[place, step, half]
+            for n in range(0, FINE, 2):
+                ref[side, slot, half, n // 2] = turn(wide, least + n)[:, 128:]
+
+    def tile(ref, side, slot, half):
+        if half is None:
+            return ref[side, slot].reshape(BLOCK, BLOCK)
+        return ref[side, slot, half].reshape(128, BLOCK)
+
+    def ahead_build(side, step):
+        step = jnp.minimum(step, PLANES - 1)
+        at = jnp.minimum(plane + step, PLANES - 1)
+        for member in range(2):
+            for place in range(2):
+                for half in range(2):
+                    wide = g_ext[member, place, at, half]
+                    for i in range(0, PARTS, 2):
+                        rows = turn(wide, -FINE * i)[:, :BLOCK]
+                        ahead[side, half, member, place, i // 2] = rows
         for place in range(2):
-            taps_of(place, h_wide[place, step], step, 0)
-            taps_of(2 + place, x_wide[place, step], step, 0)
-
-    def behind_taps(step):
+            taps_of(taps_a, side, place, h_wide, place, step, 0)
+            taps_of(taps_a, side, 2 + place, x_wide, place, step, 0)
+
+    def behind_build(side, step):
+        step = jnp.minimum(step, PLANES - 1)
+        at = jnp.maximum(plane - step, 0)
+        for member in range(2):
+            for half in range(2):
+                wide = x_ext[member, at, half]
+                for i in range(0, PARTS, 2):
+                    rows = turn(wide, -FINE * (i + 1))[:, :BLOCK]
+                    behind[side, half, member, i // 2] = rows
         for place in range(2):
-            taps_of(4 + place, f_wide[place, step], step, 1 - FINE)
-
-    size = PARTS * RING
-
-    def rhs(slot, step):
-        return taps[slot, step].reshape(BLOCK, BLOCK)
-
-    def pulled_and_cross(lhs, step):
-        high = nt_dot(lhs, rhs(0, step))
+            taps_of(taps_b, side, place, f_wide, place, step, 1 - FINE)
+
+    def pulled_and_cross(windows, rows, side, half):
+        lhs = ahead[windows, rows].reshape(4 * size, BLOCK)
+        tops = jnp.concatenate([lhs[:size], lhs[2 * size : 3 * size]], axis=0)
+        low = nt_dot(tops, tile(taps_a, side, 1, half))
+        if half is None:
+            high = nt_dot(lhs, tile(taps_a, side, 0, half))
         pulled, cross = [], None
         for member in range(2):
             at = 2 * size * member
-            low = nt_dot(lhs[at : at + size], rhs(1, step))
-            pulled.append(high[at : at + size] + high[at + size : at + 2 * size] + low)
-            both = nt_dot(lhs[at : at + 2 * size], rhs(2 + member, step))
+            part = lhs[at : at + 2 * size]
+            other = tile(taps_a, side, 2 + member, half)
+            if half is None:
+                first, both = high[at : at + 2 * size], nt_dot(part, other)
+            else:
+                wide = jnp.concatenate([tile(taps_a, side, 0, half), other], axis=0)
+                wide = nt_dot(part, wide)
+                first, both = wide[:, :128], wide[:, 128:]
+            low_part = low[size * member : size * member + size]
+            pulled.append(first[:size] + first[size:] + low_part)
             both = both[:size] + both[size:]
             cross = both if cross is None else cross + both
         return pulled[0], pulled[1], cross
 
-    def convolved(lhs, step):
-        both = nt_dot(lhs, rhs(4, step)) + nt_dot(lhs, rhs(5, step))
+    def convolved(windows, rows, side, half):
+        lhs = behind[windows, rows].reshape(2 * size, BLOCK)
+        high, low = tile(taps_b, side, 0, half), tile(taps_b, side, 1, half)
+        if half is None:
+            both = nt_dot(lhs, high) + nt_dot(lhs, low)
+        else:
+            both = nt_dot(lhs, jnp.concatenate([high, low], axis=0))
+            both = both[:, :128] + both[:, 128:]
         return both[:size], both[size:]
 
-    def ahead_step(step, first):
-        for member in range(2):
-            for place in range(2):
-                wide = g_ext[member, place, plane + step]
-                for i in range(PARTS):
-                    ahead[member, place, i] = turn(wide, -FINE * i)[:, :BLOCK]
-        lhs = ahead[...].reshape(4 * size, BLOCK)
-        if not first:
-            for k, value in enumerate(pulled_and_cross(lhs, step - 1)):
-                acc[1, 2 + k] += value
-        for k, value in enumerate(pulled_and_cross(lhs, step)):
-            if not first:
-                acc[0, 2 + k] += value
-            else:
-                acc[0, 2 + k] = value
-                acc[1, 2 + k] = jnp.zeros((size, BLOCK), F32)
-        ahead_taps(jnp.minimum(step + 1, PLANES - 1) if not first else 1)
-
-    def behind_step(step, first):
-        for member in range(2):
-            wide = x_ext[member, plane - step]
-            for i in range(PARTS):
-                behind[member, i] = turn(wide, -FINE * (i + 1))[:, :BLOCK]
-        lhs = behind[...].reshape(2 * size, BLOCK)
-        if not first:
-            for k, value in enumerate(convolved(lhs, step - 1)):
-                acc[1, k] += value
-        for k, value in enumerate(convolved(lhs, step)):
-            if not first:
-                acc[0, k] += value
-            else:
-                acc[0, k] = value
-                acc[1, k] = jnp.zeros((size, BLOCK), F32)
-        behind_taps(jnp.minimum(step + 1, PLANES - 1) if not first else 1)
-
-    ahead_taps(0)
-    behind_taps(0)
-    ahead_step(0, True)
-    behind_step(0, True)
-    def ahead_loop(step, carry):
-        ahead_step(step, False)
-        return carry
-
-    def behind_loop(step, carry):
-        behind_step(step, False)
-        return carry
-
-    lax.fori_loop(1, PLANES - plane, ahead_loop, 0)
-    lax.fori_loop(1, plane + 1, behind_loop, 0)
-
-    lanes = lax.broadcasted_iota(jnp.int32, (RING, BLOCK), 1) % FINE
+    def products(first, multiply, near_rows, side, start):
+        jobs = [(0, near_rows, side, None), (0, 1 - near_rows, side, 0)]
+        if not start:
+            jobs = [(1, 1 - near_rows, 1 - side, None), (1, near_rows, 1 - side, 1)] + jobs
+        for far, rows, taps_side, half in jobs:
+            lanes = slice(None) if half is None else slice(128 * half, 128 * half + 128)
+            for k, value in enumerate(multiply(side, rows, taps_side, half)):
+                if start:
+                    acc[far, first + k, rows, :, lanes] = value
+                else:
+                    acc[far, first + k, rows, :, lanes] += value
+        if start:
+            acc[1, first : first + (2 if first == 0 else 3)] = jnp.zeros(
+                (2 if first == 0 else 3, 2, size, BLOCK), F32
+            )
+
+    def run(first, multiply, near_rows, build, steps):
+        def pair(i, carry):
+            products(first, multiply, near_rows, 1, False)
+            build(0, 2 * i + 2)
+            products(first, multiply, near_rows, 0, False)
+            build(1, 2 * i + 3)
+            return carry
+
+        build(0, 0)
+        products(first, multiply, near_rows, 0, True)
+        build(1, 1)
+        lax.fori_loop(0, steps // 2, pair, 0)
+        pl.when(steps % 2 == 1)(lambda: products(first, multiply, near_rows, 1, False))
+
+    run(0, convolved, 0, behind_build, plane)
+    run(2, pulled_and_cross, 1, ahead_build, PLANES - 1 - plane)
+
+    lanes = lax.broadcasted_iota(jnp.int32, (RING, BLOCK), 1)
+    lanes = lanes // 128 * 8 + lanes % 8
     lines = lax.broadcasted_iota(jnp.int32, (RING, BLOCK), 0)
-    source = lax.broadcasted_iota(jnp.int32, (BLOCK, BLOCK), 0) // FINE
+    source = lax.broadcasted_iota(jnp.int32, (BLOCK, BLOCK), 0) % 128
+    source = source // 16 * 2 + source // 8 % 2
     target = lax.broadcasted_iota(jnp.int32, (BLOCK, BLOCK), 1)
     total = jnp.zeros((5 * RING, BLOCK), F32)
     for i in range(PARTS):
         pieces = []
         for k in range(5):
-            near = acc[0, k, RING * i : RING * i + RING]
-            far = acc[1, k, RING * i : RING * i + RING]
+            near, far = (
+                jnp.concatenate([acc[side, k, half, 8 * i : 8 * i + 8] for half in range(2)], axis=0)
+                for side in range(2)
+            )
             value = jnp.where(lines + lanes < RING if k < 2 else lines >= lanes, near, far)
             for bit in (1, 2, 4, 8):
                 moved = pltpu.roll(value, bit if k < 2 else RING - bit, 0)
@@ -192,15 +219,16 @@
         ],
         out_specs=pl.BlockSpec(memory_space=pltpu.VMEM),
         scratch_shapes=[
-            pltpu.VMEM((2, PLANES, RING, 384), BF16),
-            pltpu.VMEM((2, PLANES, RING, 384), BF16),
-            pltpu.VMEM((2, PLANES, RING, 384), BF16),
-            pltpu.VMEM((2, 2, PLANES, RING, 2 * BLOCK), BF16),
-            pltpu.VMEM((2, PLANES, RING, 2 * BLOCK), BF16),
-            pltpu.VMEM((6, PLANES, FINE, FINE, BLOCK), BF16),
-            pltpu.VMEM((2, 2, PARTS, RING, BLOCK), BF16),
-            pltpu.VMEM((2, PARTS, RING, BLOCK), BF16),
-            pltpu.VMEM((2, 5, PARTS * RING, BLOCK), F32),
+            pltpu.VMEM((2, PLANES, 2, 16, 384), BF16),
+            pltpu.VMEM((2, PLANES, 2, 16, 384), BF16),
+            pltpu.VMEM((2, PLANES, 2, 16, 384), BF16),
+            pltpu.VMEM((2, 2, PLANES, 2, 16, 2 * BLOCK), BF16),
+            pltpu.VMEM((2, PLANES, 2, 16, 2 * BLOCK), BF16),
+            pltpu.VMEM((2, 4, 2, FINE // 2, 16, BLOCK), BF16),
+            pltpu.VMEM((2, 2, 2, FINE // 2, 16, BLOCK), BF16),
+            pltpu.VMEM((2, 2, 2, 2, PARTS // 2, 16, BLOCK), BF16),
+            pltpu.VMEM((2, 2, 2, PARTS // 2, 16, BLOCK), BF16),
+            pltpu.VMEM((2, 5, 2, PARTS * 8, BLOCK), F32),
         ],
         compiler_params=pltpu.CompilerParams(vmem_limit_bytes=32 * 1024 * 1024),
     )(plane, arrived)

time: 87.5 us -> 86.5 us (0.989)
  Pallas kernels: 9.08 us -> 8.12 us
    pallas_call x1, Pallas kernels: 8.33 us -> 7.36 us  [middle(): pl.pallas_call(middle_kernel, out_shape=jax.ShapeDtypeStruct((10 * RING,...]
where the time goes in v10:
time: 86.5 us; the launch traced here: 86.1 us
  blocking collectives  75.9 us (88%)
  Pallas kernels  8.12 us (9%)
  local copies, waits for them, and re-layouts  1.37 us (2%)
    all_to_all x3, blocking collectives, exchange(): lax.all_to_all(rows.reshape(members, 1, -1), 'seq', split_axis=0, concat_...  54.9 us
    all_gather x1, blocking collectives, body(): every_filter = lax.all_gather(filters, 'chan', axis=0)  12 us
    all_gather x1, blocking collectives, body(): shares = lax.all_gather(sums(returned), 'chan', axis=0)  9 us
    pallas_call x1, Pallas kernels, middle(): pl.pallas_call(middle_kernel, out_shape=jax.ShapeDtypeStruct((10 * RING,...  7.36 us

profile of v10, /device:TPU:1, one launch (start us, length us, event | category | flops | bytes accessed | tf_op | source)
XLA Modules:
  0.0 86.1 jit_solution(2986872163847371448)
XLA Ops:
  0.6 0.0 copy-start.2
  0.6 12.0 %all-gather.2.filter_ref = f32[4,2,256]{2,1,0:T(2,128)S(1)} all-gather(f32[1,2,256]{2,1,0:T(2,128)} %bitcast.20), channel_id=2, replica_groups=mesh['seq'=128,'chan'=4] {'chan'}, dimensions={0}, use_global_device_ids=true | all-gather | bytes 10240 | tf_op jit(solution)/shard_map/all_gather | solution.py:353
  12.6 0.0 copy-done.2
  12.6 0.0 copy-start
  12.6 0.0 copy-start.3
  12.6 0.7 copy-done
  13.3 0.0 copy-done.3
  13.4 0.0 copy-start.1
  13.4 0.6 copy-done.1
  14.0 0.1 shard_map.76
  14.1 21.3 %all_to_all.15 = f32[16,1,1280]{2,1,0:T(1,128)S(1)} all-to-all(f32[16,1,1280]{2,1,0:T(1,128)S(1)} %bitcast.18), channel_id=1, replica_groups={{0,4,8,12,16,20,24,28,32,36,40,44,48,52,56,60},{64,68,72,76,80,84,88,92..., dimensions={0} | all-to-all | bytes 163840 | tf_op jit(solution)/shard_map/all_to_all | solution.py:337
  35.4 16.7 %all_to_all.16 = f32[8,1,20480]{2,1,0:T(1,128)S(1)} all-to-all(f32[8,1,20480]{2,1,0:T(1,128)S(1)} %bitcast.12), channel_id=1, replica_groups={{0,64,128,192,256,320,384,448},{4,68,132,196,260,324,388,452},{8,72,136..., dimensions={0} | all-to-all | bytes 1310720 | tf_op jit(solution)/shard_map/all_to_all | solution.py:337
  52.1 7.4 %shard_map.78 = f32[160,128]{1,0:T(8,128)S(1)} custom-call(s32[1]{0:T(128)} %bitcast.2.plane_ref, f32[8,10,16,128]{3,2,1,0:T(8,128)S(1)} %bitcast.11), custom_call_target="tpu_custom_call" | custom-call | tf_op jit(solution)/shard_map/pallas_call | solution.py:213
  59.5 17.0 %all_to_all.17 = f32[16,1,1280]{2,1,0:T(1,128)S(1)} all-to-all(f32[16,1,1280]{2,1,0:T(1,128)S(1)} %bitcast.15), channel_id=1, replica_groups={{0,4,8,12,16,20,24,28,32,36,40,44,48,52,56,60},{64,68,72,76,80,84,88,92..., dimensions={0} | all-to-all | bytes 163840 | tf_op jit(solution)/shard_map/all_to_all | solution.py:337
  76.5 9.0 %all-gather.1 = f32[32,256]{1,0:T(8,128)S(1)} all-gather(f32[8,256]{1,0:T(8,128)S(1)} %shard_map.79), channel_id=3, replica_groups=mesh['seq'=128,'chan'=4] {'chan'}, dimensions={0}, use_global_device_ids=true | all-gather | bytes 40960 | tf_op jit(solution)/shard_map/all_gather | solution.py:360
  85.5 0.6 shard_map.80
  (5 shorter events, 0.1 us)
Async XLA Ops:
  0.6 12.0 %copy-start.2 = (bf16[32,256]{1,0:T(8,128)(2,1)S(1)}, bf16[32,256]{1,0:T(8,128)(2,1)}, u32[]{:S(2)}) copy-start(bf16[32,256]{1,0:T(8,128)(2,1)} %param.5) | copy-start | bytes 49156
  12.6 0.7 copy-start
  12.6 0.7 copy-start.3
  13.4 0.7 copy-start.1

commit v11 on v10

--- a/solution.py
+++ b/solution.py
@@ -231,6 +231,9 @@
             pltpu.VMEM((2, 5, 2, PARTS * 8, BLOCK), F32),
         ],
         compiler_params=pltpu.CompilerParams(vmem_limit_bytes=32 * 1024 * 1024),
+        cost_estimate=pl.CostEstimate(
+            flops=2 * 116 * BLOCK**3, bytes_accessed=720 * 1024, transcendentals=0
+        ),
     )(plane, arrived)
 
 
@@ -238,7 +241,7 @@
 SMALL = pltpu.CompilerParams(vmem_limit_bytes=4 * 1024 * 1024)
 
 
-def source_kernel(signal_ref, filter_ref, skip_ref, out_ref, aside_ref):
+def source_kernel(signal_ref, filter_ref, out_ref):
     filters = jnp.concatenate([filter_ref[i] for i in range(4)] * 2, axis=0)
     line = 0
     for value in [signal_ref[RING * i : RING * i + RING] for i in range(4)] + [filters]:
@@ -246,23 +249,33 @@
             part = value[:, 128 * half : 128 * half + 128]
             out_ref[pl.ds(line, RING, stride=10), :] = part
             line += 1
+
+
+def source(signals, filters):
+    return pl.pallas_call(
+        source_kernel,
+        out_shape=jax.ShapeDtypeStruct((10 * RING, 128), F32),
+        in_specs=[VMEM] * 2,
+        out_specs=VMEM,
+        compiler_params=SMALL,
+    )(signals, filters)
+
+
+def column_kernel(skip_ref, out_ref):
     across = lax.broadcasted_iota(jnp.int32, (32, 32), 1)
     down = lax.broadcasted_iota(jnp.int32, (32, 32), 0)
     skip = jnp.where(across == down, skip_ref[...], 0.0).sum(axis=1, keepdims=True)
-    aside_ref[...] = jnp.broadcast_to(skip, aside_ref.shape)
-
-
-def source(signals, filters, skip):
-    return pl.pallas_call(
-        source_kernel,
-        out_shape=(
-            jax.ShapeDtypeStruct((10 * RING, 128), F32),
-            jax.ShapeDtypeStruct((32, BLOCK), F32),
-        ),
-        in_specs=[VMEM] * 3,
-        out_specs=[VMEM] * 2,
-        compiler_params=SMALL,
-    )(signals, filters, skip)
+    out_ref[...] = jnp.broadcast_to(skip, out_ref.shape)
+
+
+def column(skip):
+    return pl.pallas_call(
+        column_kernel,
+        out_shape=jax.ShapeDtypeStruct((32, BLOCK), F32),
+        in_specs=[VMEM],
+        out_specs=VMEM,
+        compiler_params=SMALL,
+    )(skip[None, :])
 
 
 def spread_kernel(in_ref, out_ref):
@@ -351,12 +364,13 @@
     mixed = grad_out.astype(F32) * gate_values.astype(F32)
     signals = jnp.concatenate([inputs.astype(F32), mixed], axis=0)
     every_filter = lax.all_gather(filters, "chan", axis=0)
-    leaving, skip = source(signals, every_filter, skip_weight[None, :])
+    leaving = source(signals, every_filter)
     plane = (lax.axis_index("seq") >> 4).astype(jnp.int32).reshape(1)
     slot = lax.axis_index("chan").astype(jnp.int32).reshape(1)
     leaving, plane, slot = lax.optimization_barrier((leaving, plane, slot))
     arrived = exchange(spread(exchange(leaving, rings)), planes)
-    returned = exchange(middle(arrived, plane), rings)
+    results, skip = lax.optimization_barrier((middle(arrived, plane), column(skip_weight)))
+    returned = exchange(results, rings)
     shares = lax.all_gather(sums(returned), "chan", axis=0)
     return final(slot, returned, signals, grad_out, skip, shares)
 

time: 86.5 us -> 86.7 us (level)
  blocking collectives: 75.9 us -> 59.1 us
  waiting for transfers between devices: 0 us -> 9.53 us
  starting transfers between devices: 0 us -> 6.65 us
    all_to_all x3 -> x2, blocking collectives: 54.9 us -> 38.6 us  [exchange(): lax.all_to_all(rows.reshape(members, 1, -1), 'seq', split_axis=0, concat_...]
    all_to_all x0 -> x1, waiting for transfers between devices: none -> 9.53 us  [exchange(): lax.all_to_all(rows.reshape(members, 1, -1), 'seq', split_axis=0, concat_...]
    all_to_all x0 -> x1, starting transfers between devices: none -> 6.65 us  [exchange(): lax.all_to_all(rows.reshape(members, 1, -1), 'seq', split_axis=0, concat_...]
  transfers between devices with their start and end apart: 0 -> 1, of which waited for: 0 -> 1; matrix products, arithmetic and copies ran while one was open for 0% -> 0% of each run, Pallas kernels for 0% -> 0%
where the time goes in v11:
time: 86.7 us; the launch traced here: 86.3 us
  blocking collectives  59.1 us (68%)
  waiting for transfers between devices  9.53 us (11%)
  Pallas kernels  8.96 us (10%)
  starting transfers between devices  6.65 us (8%)
    all_to_all x2, blocking collectives, exchange(): lax.all_to_all(rows.reshape(members, 1, -1), 'seq', split_axis=0, concat_...  38.6 us
    all_gather x1, blocking collectives, body(): every_filter = lax.all_gather(filters, 'chan', axis=0)  11.8 us
    all_to_all x1, waiting for transfers between devices, exchange(): lax.all_to_all(rows.reshape(members, 1, -1), 'seq', split_axis=0, concat_...  9.53 us
    all_gather x1, blocking collectives, body(): shares = lax.all_gather(sums(returned), 'chan', axis=0)  8.59 us
    pallas_call x1, Pallas kernels, middle(): pl.pallas_call(middle_kernel, out_shape=jax.ShapeDtypeStruct((10 * RING,...  7.35 us
    all_to_all x1, starting transfers between devices, exchange(): lax.all_to_all(rows.reshape(members, 1, -1), 'seq', split_axis=0, concat_...  6.65 us
  transfers between devices with their start and end apart: 1, of which 1 were waited for; matrix products, arithmetic and copies ran while one was open for 0% of the time, Pallas kernels for 0%

profile of v11, /device:TPU:1, one launch (start us, length us, event | category | flops | bytes accessed | tf_op | source)
XLA Modules:
  0.0 86.3 jit_solution(11891166496103924934)
XLA Ops:
  0.6 0.0 copy-start.3
  0.6 0.0 copy-start.2
  0.7 0.7 convert_element_type.9
  1.4 0.0 copy-start
  1.4 0.0 copy-done.3
  1.4 11.8 %all-gather.2.filter_ref = f32[4,2,256]{2,1,0:T(2,128)S(1)} all-gather(f32[1,2,256]{2,1,0:T(2,128)S(1)} %bitcast.19), channel_id=2, replica_groups=mesh['seq'=128,'chan'=4] {'chan'}, dimensions={0}, use_global_device_ids=true | all-gather | bytes 10240 | tf_op jit(solution)/shard_map/all_gather | solution.py:366
  13.2 0.0 copy-done.2
  13.2 0.0 copy-done
  13.3 21.3 %all_to_all.15 = f32[16,1,1280]{2,1,0:T(1,128)S(1)} all-to-all(f32[16,1,1280]{2,1,0:T(1,128)S(1)} %bitcast.14), channel_id=1, replica_groups={{0,4,8,12,16,20,24,28,32,36,40,44,48,52,56,60},{64,68,72,76,80,84,88,92..., dimensions={0} | all-to-all | bytes 163840 | tf_op jit(solution)/shard_map/all_to_all | solution.py:350
  34.6 0.9 %shard_map.77 = f32[8,10,16,128]{3,2,1,0:T(8,128)} custom-call(f32[160,128]{1,0:T(8,128)S(1)} %bitcast.15), custom_call_target="tpu_custom_call" | custom-call | tf_op jit(solution)/shard_map/pallas_call | solution.py:289
  35.4 6.7 %all-to-all-start.1 = ((f32[8,1,20480]{2,1,0:T(1,128)}), f32[8,1,20480]{2,1,0:T(1,128)S(1)}, u32[]{:S(2)}, u32[]{:S(2)}) async-start(f32[8,1,20480]{2,1,0:T(1,128)} %bitcast.5), calls=%async_computation.1 | async-start | bytes 1310720 | tf_op jit(solution)/shard_map/all_to_all | solution.py:350
  42.1 0.0 copy-start.1
  42.1 0.7 copy-done.1
  42.8 0.1 shard_map.79.skip_ref
  42.8 9.5 %all-to-all-done.1 = f32[8,1,20480]{2,1,0:T(1,128)S(1)} async-done(((f32[8,1,20480]{2,1,0:T(1,128)}), f32[8,1,20480]{2,1,0:T(1,128)S(1)}, u32[]{:S(2)}, u32[]{:S(2)}) %all-to-all-start.1) | async-done | bytes 655392 | tf_op jit(solution)/shard_map/all_to_all | solution.py:350
  52.4 7.4 %shard_map.78 = f32[160,128]{1,0:T(8,128)S(1)} custom-call(s32[1]{0:T(128)} %bitcast.1.plane_ref, f32[8,10,16,128]{3,2,1,0:T(8,128)S(1)} %bitcast.13), custom_call_target="tpu_custom_call" | custom-call | flops 3892314112 | bytes 737280 | tf_op jit(solution)/shard_map/pallas_call | solution.py:213
  59.7 17.4 %all_to_all.16 = f32[16,1,1280]{2,1,0:T(1,128)S(1)} all-to-all(f32[16,1,1280]{2,1,0:T(1,128)S(1)} %bitcast.17), channel_id=1, replica_groups={{0,4,8,12,16,20,24,28,32,36,40,44,48,52,56,60},{64,68,72,76,80,84,88,92..., dimensions={0} | all-to-all | bytes 163840 | tf_op jit(solution)/shard_map/all_to_all | solution.py:350
  77.1 8.6 %all-gather.1 = f32[32,256]{1,0:T(8,128)S(1)} all-gather(f32[8,256]{1,0:T(8,128)S(1)} %shard_map.80), channel_id=3, replica_groups=mesh['seq'=128,'chan'=4] {'chan'}, dimensions={0}, use_global_device_ids=true | all-gather | bytes 40960 | tf_op jit(solution)/shard_map/all_gather | solution.py:374
  85.7 0.6 shard_map.81
  (4 shorter events, 0.0 us)
Async XLA Ops:
  0.6 0.8 copy-start.3
  0.6 12.6 %copy-start.2 = (bf16[32,256]{1,0:T(8,128)(2,1)S(1)}, bf16[32,256]{1,0:T(8,128)(2,1)}, u32[]{:S(2)}) copy-start(bf16[32,256]{1,0:T(8,128)(2,1)} %param.6) | copy-start | bytes 49156
  1.4 11.8 %copy-start = (bf16[32,256]{1,0:T(8,128)(2,1)S(1)}, bf16[32,256]{1,0:T(8,128)(2,1)}, u32[]{:S(2)}) copy-start(bf16[32,256]{1,0:T(8,128)(2,1)} %up_ref.1) | copy-start | bytes 49156
  35.4 16.9 %all-to-all-start.1 = ((f32[8,1,20480]{2,1,0:T(1,128)}), f32[8,1,20480]{2,1,0:T(1,128)S(1)}, u32[]{:S(2)}, u32[]{:S(2)}) async-start(f32[8,1,20480]{2,1,0:T(1,128)} %bitcast.5), calls=%async_computation.1 | async-start | bytes 1310720 | tf_op jit(solution)/shard_map/all_to_all | solution.py:350
  42.1 0.7 copy-start.1

commit v12 on v11

--- a/solution.py
+++ b/solution.py
@@ -368,8 +368,9 @@
     plane = (lax.axis_index("seq") >> 4).astype(jnp.int32).reshape(1)
     slot = lax.axis_index("chan").astype(jnp.int32).reshape(1)
     leaving, plane, slot = lax.optimization_barrier((leaving, plane, slot))
-    arrived = exchange(spread(exchange(leaving, rings)), planes)
-    results, skip = lax.optimization_barrier((middle(arrived, plane), column(skip_weight)))
+    ring, skip = lax.optimization_barrier((exchange(leaving, rings), column(skip_weight)))
+    arrived = exchange(spread(ring), planes)
+    results = middle(arrived, plane)
     returned = exchange(results, rings)
     shares = lax.all_gather(sums(returned), "chan", axis=0)
     return final(slot, returned, signals, grad_out, skip, shares)

time: 86.7 us -> 86.7 us (level)
  blocking collectives: 59.1 us -> 54.7 us
  starting transfers between devices: 6.65 us -> 9.54 us
  waiting for transfers between devices: 9.53 us -> 11.2 us
    all_to_all x2, blocking collectives: 38.6 us -> 33.7 us  [exchange(): lax.all_to_all(rows.reshape(members, 1, -1), 'seq', split_axis=0, concat_...]
    all_to_all x1, starting transfers between devices: 6.65 us -> 9.54 us  [exchange(): lax.all_to_all(rows.reshape(members, 1, -1), 'seq', split_axis=0, concat_...]
    all_to_all x1, waiting for transfers between devices: 9.53 us -> 11.2 us  [exchange(): lax.all_to_all(rows.reshape(members, 1, -1), 'seq', split_axis=0, concat_...]
where the time goes in v12:
time: 86.7 us; the launch traced here: 86.2 us
  blocking collectives  54.7 us (63%)
  waiting for transfers between devices  11.2 us (13%)
  starting transfers between devices  9.54 us (11%)
  Pallas kernels  8.75 us (10%)
  local copies, waits for them, and re-layouts  1.37 us (2%)
    all_to_all x2, blocking collectives, exchange(): lax.all_to_all(rows.reshape(members, 1, -1), 'seq', split_axis=0, concat_...  33.7 us
    all_gather x1, blocking collectives, body(): every_filter = lax.all_gather(filters, 'chan', axis=0)  12 us
    all_to_all x1, waiting for transfers between devices, exchange(): lax.all_to_all(rows.reshape(members, 1, -1), 'seq', split_axis=0, concat_...  11.2 us
    all_to_all x1, starting transfers between devices, exchange(): lax.all_to_all(rows.reshape(members, 1, -1), 'seq', split_axis=0, concat_...  9.54 us
    all_gather x1, blocking collectives, body(): shares = lax.all_gather(sums(returned), 'chan', axis=0)  9 us
    pallas_call x1, Pallas kernels, middle(): pl.pallas_call(middle_kernel, out_shape=jax.ShapeDtypeStruct((10 * RING,...  7.36 us
  transfers between devices with their start and end apart: 1, of which 1 were waited for; matrix products, arithmetic and copies ran while one was open for 0% of the time, Pallas kernels for 0%

profile of v12, /device:TPU:1, one launch (start us, length us, event | category | flops | bytes accessed | tf_op | source)
XLA Modules:
  0.0 86.2 jit_solution(2195405429801098764)
XLA Ops:
  0.6 0.0 copy-start.2
  0.6 12.0 %all-gather.2.filter_ref = f32[4,2,256]{2,1,0:T(2,128)S(1)} all-gather(f32[1,2,256]{2,1,0:T(2,128)} %bitcast.19), channel_id=2, replica_groups=mesh['seq'=128,'chan'=4] {'chan'}, dimensions={0}, use_global_device_ids=true | all-gather | bytes 10240 | tf_op jit(solution)/shard_map/all_gather | solution.py:366
  12.6 0.0 copy-done.2
  12.6 0.0 copy-start
  12.6 0.0 copy-start.3
  12.6 0.7 copy-done
  13.3 0.0 copy-done.3
  13.4 0.6 shard_map.76
  14.0 9.5 %all-to-all-start = ((f32[16,1,1280]{2,1,0:T(1,128)}), f32[16,1,1280]{2,1,0:T(1,128)S(1)}, u32[]{:S(2)}, u32[]{:S(2)}) async-start(f32[16,1,1280]{2,1,0:T(1,128)} %bitcast.3), calls=%async_computation | async-start | bytes 163840 | tf_op jit(solution)/shard_map/all_to_all | solution.py:350
  23.6 0.0 copy-start.1
  23.6 0.6 copy-done.1
  24.2 0.1 shard_map.77.skip_ref
  24.3 11.2 %all-to-all-done = f32[16,1,1280]{2,1,0:T(1,128)S(1)} async-done(((f32[16,1,1280]{2,1,0:T(1,128)}), f32[16,1,1280]{2,1,0:T(1,128)S(1)}, u32[]{:S(2)}, u32[]{:S(2)}) %all-to-all-start) | async-done | bytes 81952 | tf_op jit(solution)/shard_map/all_to_all | solution.py:350
  35.6 16.7 %all_to_all.15 = f32[8,1,20480]{2,1,0:T(1,128)S(1)} all-to-all(f32[8,1,20480]{2,1,0:T(1,128)S(1)} %bitcast.11), channel_id=1, replica_groups={{0,64,128,192,256,320,384,448},{4,68,132,196,260,324,388,452},{8,72,136..., dimensions={0} | all-to-all | bytes 1310720 | tf_op jit(solution)/shard_map/all_to_all | solution.py:350
  52.2 7.4 %shard_map.79 = f32[160,128]{1,0:T(8,128)S(1)} custom-call(s32[1]{0:T(128)} %bitcast.1.plane_ref, f32[8,10,16,128]{3,2,1,0:T(8,128)S(1)} %bitcast.14), custom_call_target="tpu_custom_call" | custom-call | flops 3892314112 | bytes 737280 | tf_op jit(solution)/shard_map/pallas_call | solution.py:213
  59.6 17.0 %all_to_all.16 = f32[16,1,1280]{2,1,0:T(1,128)S(1)} all-to-all(f32[16,1,1280]{2,1,0:T(1,128)S(1)} %bitcast.17), channel_id=1, replica_groups={{0,4,8,12,16,20,24,28,32,36,40,44,48,52,56,60},{64,68,72,76,80,84,88,92..., dimensions={0} | all-to-all | bytes 163840 | tf_op jit(solution)/shard_map/all_to_all | solution.py:350
  76.6 9.0 %all-gather.1 = f32[32,256]{1,0:T(8,128)S(1)} all-gather(f32[8,256]{1,0:T(8,128)S(1)} %shard_map.80), channel_id=3, replica_groups=mesh['seq'=128,'chan'=4] {'chan'}, dimensions={0}, use_global_device_ids=true | all-gather | bytes 40960 | tf_op jit(solution)/shard_map/all_gather | solution.py:375
  85.6 0.6 shard_map.81
  (5 shorter events, 0.1 us)
Async XLA Ops:
  0.6 12.0 %copy-start.2 = (bf16[32,256]{1,0:T(8,128)(2,1)S(1)}, bf16[32,256]{1,0:T(8,128)(2,1)}, u32[]{:S(2)}) copy-start(bf16[32,256]{1,0:T(8,128)(2,1)} %param.5) | copy-start | bytes 49156
  12.6 0.7 copy-start
  12.6 0.7 copy-start.3
  14.0 21.5 %all-to-all-start = ((f32[16,1,1280]{2,1,0:T(1,128)}), f32[16,1,1280]{2,1,0:T(1,128)S(1)}, u32[]{:S(2)}, u32[]{:S(2)}) async-start(f32[16,1,1280]{2,1,0:T(1,128)} %bitcast.3), calls=%async_computation | async-start | bytes 163840 | tf_op jit(solution)/shard_map/all_to_all | solution.py:350
  23.6 0.7 copy-start.1
